TPU v7x, 512 devices: a whole 4x8x8 slice. The times are simulated.
512 devices in a mesh: nodes: 128 (over y, z, core), feat: 4 (over x).
Axes of the slice: x: 4, y: 8, z: 8, core: 2. Of those that a mesh axis runs over, the one named last changes fastest.
Arguments:
- features: bfloat16 [65536, 128], P('nodes', 'feat'), may hold values from -6 to 6
- band_counts: bfloat16 [512, 3, 128, 128], P('nodes'), may hold values from 0 to 3, as said below
- far_counts: bfloat16 [8192, 128, 128], P('nodes'), may hold values from 0 to 3, as said below
- far_row: int32 [8192], P('nodes'), may hold values from 0 to 3
- far_src: int32 [8192], P('nodes'), may hold values from 0 to 127, as said below
- export_block: int32 [128], P('nodes'), may hold values from 0 to 3
- w_self: bfloat16 [128, 256], P('feat'), may hold values from -0.375 to 0.375
- w_neigh: bfloat16 [128, 256], P('feat'), may hold values from -0.375 to 0.375
- bias: float32 [256], P('feat'), may hold values from -3 to 3
- cotangent: bfloat16 [65536, 256], P('nodes', 'feat')
Outputs:
- hidden: bfloat16 [65536, 256], P('nodes', 'feat')
- grad_features: bfloat16 [65536, 128], P('nodes', 'feat')
- grad_self: float32 [128, 256], P('feat')
- grad_neigh: float32 [128, 256], P('feat')
- grad_bias: float32 [256], P('feat')
Inputs may be any that keep to these rules, and one draw needn't show every extreme that they name: Whole numbers; the diagonal of band_counts[g, 1] is at least 1; blocks that would lie outside the slab (band_counts[0, 0] and band_counts[511, 2]) are zero. `far_counts`: whole numbers. far_src[f] differs from the index of nodes that holds block f, f // 64; the 64 blocks of one index of nodes name 64 different sources.
All inputs are finite; a program needn't handle non-finite values.
Results may differ from a plain program's by a relative error of at most 0.0044.
The roundings to bfloat16 on the way count: a program that leaves them out, or rounds other values in their place, can miss the bound.
Values may be sent and summed in bfloat16 or wider, within the bound.
A program may use at most 64 MiB of HBM per device.

v0:
```python
import jax
import jax.numpy as jnp
from jax import lax
from jax.sharding import PartitionSpec as P


def padded_2(cells, sides, width):
    for axis, dim in sides:
        count = lax.axis_size(axis)
        ends = count - 1
        head = lax.slice_in_dim(cells, 0, width, axis=dim)
        tail = lax.slice_in_dim(cells, cells.shape[dim] - width, cells.shape[dim], axis=dim)
        cells = jnp.concatenate(
            [
                lax.ppermute(tail, axis, [(i, (i + 1) % count) for i in range(ends)]),
                cells,
                lax.ppermute(head, axis, [((i + 1) % count, i) for i in range(ends)]),
            ],
            axis=dim,
        )
    return cells


def on_device(
    features,
    band_counts,
    far_counts,
    far_row,
    far_src,
    export_block,
    w_self,
    w_neigh,
    bias,
    cotangent,
):
    high = lax.Precision.HIGHEST
    row_count, col_count = features.shape
    blk_count = band_counts.shape[0]
    blk_size = band_counts.shape[2]
    node_count = lax.axis_size("nodes")
    padded = padded_2(features, (("nodes", 0),), blk_size)
    near = padded.reshape(blk_count + 2, blk_size, col_count)
    window = jnp.stack([near[0:blk_count], near[1 : blk_count + 1], near[2 : blk_count + 2]], 1)
    summed = jnp.einsum("bkij,bkjc->bic", band_counts, window, preferred_element_type=jnp.float32)
    own_blocks = features.reshape(blk_count, blk_size, col_count)
    chosen = lax.dynamic_index_in_dim(own_blocks, export_block[0], 0, keepdims=True)
    exported = lax.all_gather(chosen, "nodes", axis=0, tiled=True)
    far_rows = exported[far_src]
    far_terms = jnp.einsum("fij,fjc->fic", far_counts, far_rows, preferred_element_type=jnp.float32)
    place = (far_row[None, :] == jnp.arange(blk_count)[:, None]).astype(jnp.float32)
    summed = summed + jnp.einsum("bf,fic->bic", place, far_terms, precision=high)
    far_degree = jnp.sum(far_counts, axis=2, dtype=jnp.float32)
    degree = jnp.sum(band_counts, axis=(1, 3), dtype=jnp.float32) + jnp.dot(
        place, far_degree, precision=high
    )
    degree_rows = degree.reshape(row_count, 1)
    aggregate = (summed.reshape(row_count, col_count) / degree_rows).astype(jnp.bfloat16)
    hid_local = bias.shape[0]
    full_inputs, full_aggregate = (
        lax.all_gather(features, "feat", axis=1, tiled=True),
        lax.all_gather(aggregate, "feat", axis=1, tiled=True),
    )
    full_self, full_neigh = (
        lax.all_gather(w_self, "feat", axis=0, tiled=True),
        lax.all_gather(w_neigh, "feat", axis=0, tiled=True),
    )
    first_col = lax.axis_index("feat") * hid_local
    self_cols = lax.dynamic_slice_in_dim(full_self, first_col, hid_local, 1)
    neigh_cols = lax.dynamic_slice_in_dim(full_neigh, first_col, hid_local, 1)
    pre = jnp.dot(full_inputs, self_cols, preferred_element_type=jnp.float32) + jnp.dot(
        full_aggregate, neigh_cols, preferred_element_type=jnp.float32
    )
    pre = pre + bias
    sigma = jax.nn.sigmoid(pre)
    hidden = (pre * sigma).astype(jnp.bfloat16)
    grad_pre = cotangent.astype(jnp.float32) * sigma * (1.0 + pre * (1.0 - sigma))
    grad_low = grad_pre.astype(jnp.bfloat16)
    bias_part = jnp.sum(grad_pre, 0)
    contract_cols = (((1,), (1,)), ((), ()))
    contract_rows = (((0,), (0,)), ((), ()))
    portion = lax.all_gather(grad_low, "feat", axis=1, tiled=True)
    self_acc = lax.dot_general(portion, w_self, contract_cols, preferred_element_type=jnp.float32)
    neigh_acc = lax.dot_general(portion, w_neigh, contract_cols, preferred_element_type=jnp.float32)
    self_grad = lax.dot_general(
        features, portion, contract_rows, preferred_element_type=jnp.float32
    )
    neigh_grad = lax.dot_general(
        aggregate, portion, contract_rows, preferred_element_type=jnp.float32
    )
    self_term, neigh_term, self_grad, neigh_grad = (self_acc, neigh_acc, self_grad, neigh_grad)
    grad_self, grad_neigh, grad_bias = lax.psum((self_grad, neigh_grad, bias_part), "nodes")
    scaled = (neigh_term / degree_rows).astype(jnp.bfloat16).reshape(blk_count, blk_size, col_count)
    back = jnp.einsum("bkij,bic->bkjc", band_counts, scaled, preferred_element_type=jnp.float32)
    empty = jnp.zeros((1, blk_size, col_count), jnp.float32)
    spread = (
        jnp.concatenate([back[:, 0], empty, empty], 0)
        + jnp.concatenate([empty, back[:, 1], empty], 0)
        + jnp.concatenate([empty, empty, back[:, 2]], 0)
    )
    outward = jnp.concatenate([spread[0], spread[blk_count + 1]], 0)
    returned = padded_2(outward.astype(jnp.bfloat16), (("nodes", 0),), blk_size).astype(
        outward.dtype
    )
    inner = spread[1 : blk_count + 1]
    inner = inner.at[0].add(returned[:blk_size])
    inner = inner.at[blk_count - 1].add(returned[3 * blk_size :])
    far_back = jnp.einsum(
        "fij,fic->fjc", far_counts, scaled[far_row], preferred_element_type=jnp.float32
    )
    owner = (far_src[:, None] == jnp.arange(node_count)[None, :]).astype(jnp.float32)
    slots = jnp.einsum("fp,fjc->pjc", owner, far_back, precision=high)
    received = lax.all_to_all(
        slots.astype(jnp.bfloat16), "nodes", split_axis=0, concat_axis=0, tiled=True
    ).astype(slots.dtype)
    far_total = jnp.sum(received, 0)
    target = (jnp.arange(blk_count) == export_block[0]).astype(jnp.float32)
    inner = inner + target[:, None, None] * far_total[None]
    grad_features = (self_term + inner.reshape(row_count, col_count)).astype(jnp.bfloat16)
    return (hidden, grad_features, grad_self, grad_neigh, grad_bias)


def solution(mesh):
    return jax.shard_map(
        on_device,
        mesh=mesh,
        in_specs=(
            P("nodes", "feat"),
            P("nodes", None, None, None),
            P("nodes", None, None),
            P("nodes"),
            P("nodes"),
            P("nodes"),
            P("feat", None),
            P("feat", None),
            P("feat"),
            P("nodes", "feat"),
        ),
        out_specs=(
            P("nodes", "feat"),
            P("nodes", "feat"),
            P("feat", None),
            P("feat", None),
            P("feat"),
        ),
        check_vma=False,
    )
```

profile of v0, /device:TPU:1, one launch (start us, length us, event | category | flops | bytes accessed | tf_op | source)
XLA Modules:
  0.0 340.0 jit_solution(1067046048478962258)
XLA Ops:
  10.1 5.4 %collective-permute-start = (bf16[128,32]{0,1:T(8,128)(2,1)S(1)}, bf16[128,32]{0,1:T(8,128)(2,1)S(1)}, u32[]{:S(2)}, u32[]{:S(2)}) collective-permute-start(bf16[128,32]{0,1:T(8,128)(2,1)S(1)} %get-tuple-element.44), channel_id=1, source_target_pairs={{0,4},{4,8},{8,12},{12,16},{16,20},{20,24},{24,28},{28,32},{32,36}... | collective-permute-start | bytes 24584 | tf_op jit(solution)/shard_map/ppermute | solution.py:15
  15.4 4.7 %collective-permute-start.1 = (bf16[128,32]{0,1:T(8,128)(2,1)S(1)}, bf16[128,32]{0,1:T(8,128)(2,1)S(1)}, u32[]{:S(2)}, u32[]{:S(2)}) collective-permute-start(bf16[128,32]{0,1:T(8,128)(2,1)S(1)} %get-tuple-element.45), channel_id=1, source_target_pairs={{4,0},{8,4},{12,8},{16,12},{20,16},{24,20},{28,24},{32,28},{36,32}... | collective-permute-start | bytes 24584 | tf_op jit(solution)/shard_map/ppermute | solution.py:17
  20.1 9.4 %all_gather.18 = bf16[128,256]{1,0:T(8,128)(2,1)S(1)} all-gather(bf16[32,256]{1,0:T(8,128)(2,1)} %param.20), channel_id=1, replica_groups=mesh['nodes'=128,'feat'=4] {'feat'}, dimensions={0}, use_global_device_ids=true | all-gather | bytes 81920 | tf_op jit(solution)/shard_map/all_gather | solution.py:64
  29.5 9.3 %all_gather.19 = bf16[512,128]{0,1:T(8,128)(2,1)S(1)} all-gather(bf16[512,32]{0,1:T(8,128)(2,1)} %param.14), channel_id=1, replica_groups=mesh['nodes'=128,'feat'=4] {'feat'}, dimensions={1}, use_global_device_ids=true | all-gather | bytes 163840 | tf_op jit(solution)/shard_map/all_gather | solution.py:60
  40.2 1.1 convert_reduce_fusion.2
  41.3 2.2 convert_reduce_fusion
  44.0 9.2 %all_gather.22 = bf16[128,256]{1,0:T(8,128)(2,1)S(1)} all-gather(bf16[32,256]{1,0:T(8,128)(2,1)S(1)} %copy-done.4), channel_id=1, replica_groups=mesh['nodes'=128,'feat'=4] {'feat'}, dimensions={0}, use_global_device_ids=true | all-gather | bytes 81920 | tf_op jit(solution)/shard_map/all_gather | solution.py:65
  53.3 43.5 %all-gather.2.cloned.1.call-done = bf16[128,128,32]{1,2,0:T(8,128)(2,1)} async-done(((bf16[1,128,32]{1,2,0:T(8,128)(2,1)}), bf16[128,128,32]{1,2,0:T(8,128)(2,1)}) %all-gather.2.cloned.1.call-update) | async-done | bytes 1048592 | tf_op jit(solution)/shard_map/all_gather | solution.py:47
  96.8 1.9 gather_fusion
  98.8 1.2 convolution_bitcast_fusion.1
  101.3 9.9 %all_gather.21 = bf16[512,128]{0,1:T(8,128)(2,1)S(1)} all-gather(bf16[512,32]{0,1:T(8,128)(2,1)S(1)} %fusion.15), channel_id=1, replica_groups=mesh['nodes'=128,'feat'=4] {'feat'}, dimensions={1}, use_global_device_ids=true | all-gather | bytes 163840 | tf_op jit(solution)/shard_map/all_gather | solution.py:61
  111.1 1.6 fusion.32
  112.7 9.4 %all_gather.23 = bf16[512,256]{0,1:T(8,128)(2,1)S(1)} all-gather(bf16[512,64]{0,1:T(8,128)(2,1)S(1)} %get-tuple-element.33), channel_id=1, replica_groups=mesh['nodes'=128,'feat'=4] {'feat'}, dimensions={1}, use_global_device_ids=true | all-gather | bytes 327680 | tf_op jit(solution)/shard_map/all_gather | solution.py:81
  123.6 1.7 convolution_convert_fusion
  125.3 1.7 copy.55
  127.0 13.5 %all-to-all-start = ((bf16[128,128,32]{1,2,0:T(8,128)(2,1)}), bf16[128,128,32]{1,2,0:T(8,128)(2,1)S(1)}, u32[]{:S(2)}, u32[]{:S(2)}) async-start(bf16[128,128,32]{1,2,0:T(8,128)(2,1)} %copy.55), calls=%async_computation | async-start | bytes 2097152 | tf_op jit(solution)/shard_map/all_to_all | solution.py:112
  140.9 2.8 collective-permute-start.3
  143.7 2.8 collective-permute-start.2
  148.1 2.0 collective-permute-done.3
  150.1 20.9 %all-to-all-done = bf16[128,128,32]{1,2,0:T(8,128)(2,1)S(1)} async-done(((bf16[128,128,32]{1,2,0:T(8,128)(2,1)}), bf16[128,128,32]{1,2,0:T(8,128)(2,1)S(1)}, u32[]{:S(2)}, u32[]{:S(2)}) %all-to-all-start) | async-done | bytes 1048608 | tf_op jit(solution)/shard_map/all_to_all | solution.py:112
  171.9 157.3 %all-reduce.5.cloned.1.call-done = (f32[32,256]{1,0:T(8,128)}, f32[32,256]{1,0:T(8,128)}, f32[64]{0:T(128)}) async-done(((f32[32,256]{1,0:T(8,128)}, f32[32,256]{1,0:T(8,128)}, f32[64]{0:T(128)}), (f32[32,256]{1,0:T(8,128)}, f32[32,256]{1,0:T(8,128)}, f32[64]{0:T(128)})) %all-reduce.5.cloned.1.call-update) | async-done | bytes 65808 | tf_op jit(solution)/shard_map/psum | solution.py:91
  329.2 1.4 copy.82
  330.6 1.4 copy.83
  332.0 1.1 copy.84
  (63 shorter events, 9.7 us)
Async XLA Ops:
  7.2 46.0 %copy-start.2 = (bf16[512,32]{0,1:T(8,128)(2,1)S(1)}, bf16[512,32]{0,1:T(8,128)(2,1)}, u32[]{:S(2)}) copy-start(bf16[512,32]{0,1:T(8,128)(2,1)} %param.14) | copy-start | bytes 98308
  7.2 36.4 %copy-start.5 = (s32[64]{0:T(128)S(1)}, s32[64]{0:T(128)}, u32[]{:S(2)}) copy-start(s32[64]{0:T(128)} %param.17) | copy-start | bytes 772
  7.2 36.8 %copy-start.4 = (bf16[32,256]{1,0:T(8,128)(2,1)S(1)}, bf16[32,256]{1,0:T(8,128)(2,1)}, u32[]{:S(2)}) copy-start(bf16[32,256]{1,0:T(8,128)(2,1)} %param.21) | copy-start | bytes 49156
  7.2 89.6 %all-gather.2.cloned.1.call-start = ((), (), s32[]{:S(2)}) async-start(), calls=%async_computation.1 | async-start | bytes 1056768 | tf_op jit(solution)/shard_map/all_gather | solution.py:47
  10.1 43.2 %collective-permute-start = (bf16[128,32]{0,1:T(8,128)(2,1)S(1)}, bf16[128,32]{0,1:T(8,128)(2,1)S(1)}, u32[]{:S(2)}, u32[]{:S(2)}) collective-permute-start(bf16[128,32]{0,1:T(8,128)(2,1)S(1)} %get-tuple-element.44), channel_id=1, source_target_pairs={{0,4},{4,8},{8,12},{12,16},{16,20},{20,24},{24,28},{28,32},{32,36}... | collective-permute-start | bytes 24584 | tf_op jit(solution)/shard_map/ppermute | solution.py:15
  15.4 37.8 %collective-permute-start.1 = (bf16[128,32]{0,1:T(8,128)(2,1)S(1)}, bf16[128,32]{0,1:T(8,128)(2,1)S(1)}, u32[]{:S(2)}, u32[]{:S(2)}) collective-permute-start(bf16[128,32]{0,1:T(8,128)(2,1)S(1)} %get-tuple-element.45), channel_id=1, source_target_pairs={{4,0},{8,4},{12,8},{16,12},{20,16},{24,20},{28,24},{32,28},{36,32}... | collective-permute-start | bytes 24584 | tf_op jit(solution)/shard_map/ppermute | solution.py:17
  53.3 45.4 %copy-start = (bf16[64,128,128]{2,1,0:T(8,128)(2,1)S(1)}, bf16[64,128,128]{2,1,0:T(8,128)(2,1)}, u32[]{:S(2)}) copy-start(bf16[64,128,128]{2,1,0:T(8,128)(2,1)} %param.16) | copy-start | bytes 6291460
  98.7 2.3 copy-start.1
  98.7 12.4 %copy-start.7 = (bf16[512,64]{0,1:T(8,128)(2,1)S(1)}, bf16[512,64]{0,1:T(8,128)(2,1)}, u32[]{:S(2)}) copy-start(bf16[512,64]{0,1:T(8,128)(2,1)} %param.23) | copy-start | bytes 196612
  98.7 12.4 %copy-start.8 = (f32[64]{0:T(128)S(1)}, f32[64]{0:T(128)}, u32[]{:S(2)}) copy-start(f32[64]{0:T(128)} %param.22) | copy-start | bytes 772
  122.9 0.7 copy-start.6
  127.0 44.0 %all-to-all-start = ((bf16[128,128,32]{1,2,0:T(8,128)(2,1)}), bf16[128,128,32]{1,2,0:T(8,128)(2,1)S(1)}, u32[]{:S(2)}, u32[]{:S(2)}) async-start(bf16[128,128,32]{1,2,0:T(8,128)(2,1)} %copy.55), calls=%async_computation | async-start | bytes 2097152 | tf_op jit(solution)/shard_map/all_to_all | solution.py:112
  140.5 30.6 %copy-start.3 = (bf16[32,256]{1,0:T(8,128)(2,1)S(1)}, bf16[32,256]{1,0:T(8,128)(2,1)}, u32[]{:S(2)}) copy-start(bf16[32,256]{1,0:T(8,128)(2,1)} %param.20) | copy-start | bytes 49156
  140.5 188.7 %all-reduce.5.cloned.1.call-start = ((), (), s32[]{:S(2)}) async-start(), calls=%async_computation.2 | async-start | bytes 132096 | tf_op jit(solution)/shard_map/psum | solution.py:91
  140.9 9.2 %collective-permute-start.3 = (bf16[128,32]{0,1:T(8,128)(2,1)S(1)}, bf16[128,32]{0,1:T(8,128)(2,1)S(1)}, u32[]{:S(2)}, u32[]{:S(2)}) collective-permute-start(bf16[128,32]{0,1:T(8,128)(2,1)S(1)} %get-tuple-element.41), channel_id=1, source_target_pairs={{4,0},{8,4},{12,8},{16,12},{20,16},{24,20},{28,24},{32,28},{36,32}... | collective-permute-start | bytes 24584 | tf_op jit(solution)/shard_map/ppermute | solution.py:17
  143.7 6.4 %collective-permute-start.2 = (bf16[128,32]{0,1:T(8,128)(2,1)S(1)}, bf16[128,32]{0,1:T(8,128)(2,1)S(1)}, u32[]{:S(2)}, u32[]{:S(2)}) collective-permute-start(bf16[128,32]{0,1:T(8,128)(2,1)S(1)} %get-tuple-element.40), channel_id=1, source_target_pairs={{0,4},{4,8},{8,12},{12,16},{16,20},{20,24},{24,28},{28,32},{32,36}... | collective-permute-start | bytes 24584 | tf_op jit(solution)/shard_map/ppermute | solution.py:15
Sparse Core Ops, SparseCore 0:
  11.6 85.1 all-gather.1
  148.2 180.9 all-reduce.4
where the time goes:
time: 341 us; the launch traced here: 340 us
  waiting for transfers between devices  224 us (66%)
  blocking collectives  47.1 us (14%)
  starting transfers between devices  29.2 us (9%)
  between operations  15 us (4%)
  local copies, waits for them, and re-layouts  10.4 us (3%)
  matrix products  9.55 us (3%)
  other arithmetic  4.96 us (1%)
    psum x1, waiting for transfers between devices, on_device(): lax.psum((self_grad, neigh_grad, bias_part), 'nodes')  157 us
    all_gather x1, waiting for transfers between devices, on_device(): exported = lax.all_gather(chosen, 'nodes', axis=0, tiled=True)  43.5 us
    all_to_all x1, waiting for transfers between devices, on_device(): lax.all_to_all(slots.astype(jnp.bfloat16), 'nodes', split_axis=0, concat_...  20.9 us
    all_to_all x1, starting transfers between devices, on_device(): lax.all_to_all(slots.astype(jnp.bfloat16), 'nodes', split_axis=0, concat_...  13.5 us
    all_gather x1, blocking collectives, on_device(): lax.all_gather(aggregate, 'feat', axis=1, tiled=True)  9.85 us
    all_gather x1, blocking collectives, on_device(): lax.all_gather(w_self, 'feat', axis=0, tiled=True)  9.39 us
    all_gather x1, blocking collectives, on_device(): portion = lax.all_gather(grad_low, 'feat', axis=1, tiled=True)  9.36 us
    all_gather x1, blocking collectives, on_device(): lax.all_gather(features, 'feat', axis=1, tiled=True)  9.31 us
  transfers between devices with their start and end apart: 7, of which 4 were waited for; matrix products, arithmetic and copies ran while one was open for 3% of the time, Pallas kernels for 0%

commit v1 on v0

v1 whole, which is shorter than its diff:
```python
import jax
import jax.numpy as jnp
from jax import lax
from jax.experimental import pallas as pl
from jax.experimental.pallas import tpu as pltpu
from jax.sharding import PartitionSpec as P

MESH = pl.DeviceIdType.MESH
F32 = jnp.float32
BF16 = jnp.bfloat16
LANES = 128
CORES = 2


def sides(nodes):
    chips = nodes // CORES
    z = 1
    while z * z < chips:
        z *= 2
    return chips // z, z


def dot(a, b, ca, cb, precision=None):
    return lax.dot_general(a, b, (((ca,), (cb,)), ((), ())), precision=precision, preferred_element_type=F32)


def eye(n, dtype):
    rows = lax.broadcasted_iota(jnp.int32, (n, n), 0)
    cols = lax.broadcasted_iota(jnp.int32, (n, n), 1)
    return jnp.where(rows == cols, 1.0, 0.0).astype(dtype)


def each(count, body):
    def step(i, carry):
        body(i)
        return carry

    lax.fori_loop(0, count, step, 0)


def nearest(i, size):
    k = i // 2 + 1
    return k + (i % 2) * (size - 2 * k)


class Stage:
    def __init__(self, send_sems, recv_sems, base, count, to, landing):
        self.send_sems, self.recv_sems, self.base, self.count = send_sems, recv_sems, base, count
        self.to, self.landing = to, landing

    def copy(self, i, dst=None):
        src, there, device = self.to(i)
        return pltpu.make_async_remote_copy(
            src_ref=src,
            dst_ref=there if dst is None else dst,
            send_sem=self.send_sems.at[self.base + i],
            recv_sem=self.recv_sems.at[self.base + i],
            device_id=device,
            device_id_type=MESH,
        )

    def start(self, i):
        self.copy(i).start()

    def arrive(self, i):
        self.copy(i, self.landing(i)).wait_recv()

    def start_all(self):
        each(self.count, self.start)

    def arrive_all(self):
        each(self.count, self.arrive)

    def drain(self):
        each(self.count, lambda i: self.copy(i).wait_send())


def make_kernel(ys, zs, xs, far, hid):
    nodes = ys * zs * CORES
    chips = ys * zs
    blks = xs
    half = 16
    cf = 2 * half
    ch = hid // xs
    fin = cf * xs
    groups = zs * CORES
    lane_groups = hid // LANES
    tiles = 2 * (cf // 8) * lane_groups
    per = tiles // groups
    sem_plan = {}

    def plan(name, count):
        base = sum(c for _, c in sem_plan.values())
        sem_plan[name] = (base, count)

    for name, count in (
        ("a0", zs - 1), ("a1", ys - 1), ("b0", ys - 1), ("b1", zs - 1), ("c0", ys), ("c1", zs),
        ("halo", 2), ("xq", xs - 1), ("cq", xs - 1), ("ws", xs - 1), ("wn", xs - 1), ("bias", xs - 1),
        ("agg", xs - 1), ("scaled", xs - 1), ("self", xs - 1), ("hid", xs - 1), ("gx", xs - 1),
        ("ga", groups - 1), ("gy", ys - 1), ("gz", groups - 1),
        ("core0", ys), ("core1", zs), ("p0", ys - 1), ("p1", zs - 1), ("r0", zs - 1), ("r1", ys - 1), ("out", 2),
    ):
        plan(name, count)
    n_sems = sum(c for _, c in sem_plan.values())

    scratch = dict(
        XT=((blks, cf, LANES), BF16), xq=((xs, cf, LANES), BF16),
        cT=((blks, ch, LANES), BF16), cq=((xs, ch, LANES), BF16),
        wsF=((xs, cf, hid), BF16), wnF=((xs, cf, hid), BF16), biasF=((xs, ch, LANES), F32),
        wsT=((hid, fin), BF16), wnT=((hid, fin), BF16), pre0=((hid, LANES), F32),
        e0=((CORES, chips, half, LANES), BF16), e1=((CORES, chips, half, LANES), BF16),
        halo=((2, cf, LANES), BF16),
        A=((LANES, far * LANES), BF16), band=((blks, 3, LANES, LANES), BF16),
        Lm=((blks * cf + half, far * LANES), BF16),
        near=((blks, cf + half, LANES), F32), deg=((blks, 8, LANES), F32),
        agg=((blks, cf, LANES), BF16), aq=((xs, cf, LANES), BF16),
        ss=((xs, cf, LANES), BF16), sq=((blks, cf, LANES), BF16),
        st=((xs, cf, LANES), F32), stq=((blks, cf, LANES), F32),
        hs=((xs, ch, LANES), BF16), hq=((blks, ch, LANES), BF16),
        gx=((xs, tiles + 1, 8, LANES), F32), gxr=((xs, tiles + 1, 8, LANES), F32),
        ga=((groups, per + 1, 8, LANES), F32), gar=((groups, per + 1, 8, LANES), F32),
        gb=((per + 1, 8, LANES), F32), gyr=((ys, per + 1, 8, LANES), F32),
        gt=((per, 8, LANES), F32), gzr=((groups, per, 8, LANES), F32),
        BK=((far, cf, LANES), F32),
        cs0=((chips, half, LANES), F32), cs1=((chips, half, LANES), F32),
        cr0=((chips, half, LANES), F32), cr1=((chips, half, LANES), F32),
        ps0=((chips, half, LANES), BF16), ps1=((chips, half, LANES), BF16),
        pr0=((ys, zs, half, LANES), BF16), pr1=((zs, ys, half, LANES), BF16),
        q0=((zs, half, LANES), F32), q1=((ys, half, LANES), F32),
        f0=((zs, half, LANES), F32), f1=((ys, half, LANES), F32),
        ho=((2, cf, LANES), F32), hr=((2, cf, LANES), F32),
        inner=((blks, cf, LANES), F32),
    )
    names = list(scratch)

    def kernel(
        row_s, src_s, inv_s, eb_s, feat_ref, ws_ref, wn_ref, bias_ref, cot_ref, band_hbm, far_hbm,
        hid_o, gf_o, gt_o, gb_o, *rest,
    ):
        s = dict(zip(names, rest))
        send_sems, recv_sems, far_sem, band_sem = rest[len(names):]
        n = lax.axis_index("nodes")
        x = lax.axis_index("feat")
        c = n % CORES
        z = (n // CORES) % zs
        y = n // (CORES * zs)
        o = 1 - c
        g_me = z * CORES + c

        def node(yy, zz, cc):
            return (yy * zs + zz) * CORES + cc

        def stage(name, to, landing):
            base, count = sem_plan[name]
            return Stage(send_sems, recv_sems, base, count, to, landing)

        def along_z(name, src, there, here):
            def to(i):
                d = nearest(i, zs)
                peer = (z + d) % zs
                return src(peer), there(z), (node(y, peer, c), x)

            return stage(name, to, lambda i: here((z - nearest(i, zs) + zs) % zs))

        def along_y(name, src, there, here):
            def to(i):
                d = nearest(i, ys)
                peer = (y + d) % ys
                return src(peer), there(y), (node(peer, z, c), x)

            return stage(name, to, lambda i: here((y - nearest(i, ys) + ys) % ys))

        def along_x(name, src, land):
            def to(i):
                peer = (x + i + 1) % xs
                return src(peer), land(x), (n, peer)

            return stage(name, to, lambda i: land((x - i - 1 + xs) % xs))

        def along_group(name, src, land):
            def to(i):
                peer = (g_me + i + 1) % groups
                return src(peer), land(g_me), (node(y, peer // CORES, peer % CORES), x)

            return stage(name, to, lambda i: land((g_me - i - 1 + groups) % groups))

        left, right = (n + nodes - 1) % nodes, (n + 1) % nodes

        def to_sides(name, first, last, land):
            def to(i):
                return (first, last)[i], land((1, 0)[i]), ((left, right)[i], x)

            class Sides(Stage):
                def start_all(self):
                    self.start(0)
                    self.start(1)

                def arrive_all(self):
                    self.arrive(0)
                    self.arrive(1)

                def drain(self):
                    for i in range(2):
                        self.copy(i).wait_send()

            base, count = sem_plan[name]
            return Sides(send_sems, recv_sems, base, count, to, lambda i: land((1, 0)[i]))

        def to_core(name, src, there, here):
            return stage(name, lambda i: (src(i), there(i), (node(y, z, o), x)), here)

        def start_far(f):
            cols = pl.ds(pl.multiple_of(f * LANES, LANES), LANES)
            pltpu.make_async_copy(far_hbm.at[f], s["A"].at[:, cols], far_sem).start()

        each(far, start_far)
        band_copy = pltpu.make_async_copy(band_hbm, s["band"], band_sem)
        band_copy.start()

        barrier = pltpu.get_barrier_semaphore()

        def greet(device):
            pl.semaphore_signal(barrier, inc=1, device_id=device, device_id_type=MESH)

        each(ys - 1, lambda i: greet((node((y + i + 1) % ys, z, c), x)))

        def greet_group(i):
            peer = (g_me + i + 1) % groups
            greet((node(y, peer // CORES, peer % CORES), x))

        each(groups - 1, greet_group)
        each(xs - 1, lambda i: greet((n, (x + i + 1) % xs)))
        greet((left, x))
        greet((right, x))

        eye_f = eye(cf, BF16)
        eye_h = eye(ch, BF16)
        for b in range(blks):
            rows = slice(b * LANES, (b + 1) * LANES)
            s["XT"][b] = dot(eye_f, feat_ref[rows, :], 1, 1).astype(BF16)
        eb = eb_s[0]
        mine = s["XT"][eb]
        s["e0"][c, y * zs + z] = mine[:half]
        s["e1"][c, z * ys + y] = mine[half:]
        for b in range(blks):
            rows = slice(b * LANES, (b + 1) * LANES)
            s["cT"][b] = dot(eye_h, cot_ref[rows, :], 1, 1).astype(BF16)

        pl.semaphore_wait(barrier, ys - 1 + groups - 1 + xs - 1 + 2)

        e0, e1 = s["e0"], s["e1"]
        a0 = along_z("a0", lambda p: e0.at[c, y * zs + z], lambda q: e0.at[c, y * zs + q], lambda q: e0.at[c, y * zs + q])
        a1 = along_y("a1", lambda p: e1.at[c, z * ys + y], lambda q: e1.at[c, z * ys + q], lambda q: e1.at[c, z * ys + q])
        a0.start_all()
        a1.start_all()
        halo = to_sides("halo", s["XT"].at[0], s["XT"].at[blks - 1], lambda i: s["halo"].at[i])
        halo.start_all()
        xq = along_x("xq", lambda p: s["XT"].at[p], lambda q: s["xq"].at[q])
        ws = along_x("ws", lambda p: ws_ref, lambda q: s["wsF"].at[q])
        wn = along_x("wn", lambda p: wn_ref, lambda q: s["wnF"].at[q])
        bias = along_x("bias", lambda p: bias_ref, lambda q: s["biasF"].at[q])
        cq = along_x("cq", lambda p: s["cT"].at[p], lambda q: s["cq"].at[q])
        early = (xq, ws, wn, bias, cq)
        for one in early:
            one.start_all()
        s["xq"][x] = s["XT"][x]
        s["cq"][x] = s["cT"][x]
        s["wsF"][x] = ws_ref[...]
        s["wnF"][x] = wn_ref[...]
        s["biasF"][x] = bias_ref[...]

        def row0(q):
            return e0.at[c, pl.ds(q * zs, zs)]

        def row1(q):
            return e1.at[c, pl.ds(q * ys, ys)]

        b0 = along_y("b0", lambda p: row0(y), row0, row0)
        b1 = along_z("b1", lambda p: row1(z), row1, row1)

        def near_y(i):
            return (y - nearest(i - 1, ys) * jnp.minimum(i, 1) + ys) % ys

        def near_z(i):
            return (z - nearest(i - 1, zs) * jnp.minimum(i, 1) + zs) % zs

        c0 = to_core(
            "c0", lambda i: row0(near_y(i)), lambda i: row0(near_y(i)), lambda i: e0.at[o, pl.ds(near_y(i) * zs, zs)]
        )
        c1 = to_core(
            "c1", lambda i: row1(near_z(i)), lambda i: row1(near_z(i)), lambda i: e1.at[o, pl.ds(near_z(i) * ys, ys)]
        )
        a0.arrive_all()
        b0.start_all()
        c0.start(0)
        a1.arrive_all()
        b1.start_all()
        c1.start(0)

        band_copy.wait()
        halo.arrive_all()
        ones = jnp.ones((half, LANES), BF16)
        for b in range(blks):
            total = None
            for k in range(3):
                w = b + k - 1
                block = s["halo"][0] if w < 0 else s["halo"][1] if w >= blks else s["XT"][w]
                term = dot(jnp.concatenate([block, ones], 0), s["band"][b, k], 1, 1)
                total = term if total is None else total + term
            s["near"][b] = total
        for one in early:
            one.arrive_all()
        eye_w = eye(hid, BF16)
        w_self = s["wsF"][...].reshape(fin, hid)
        w_neigh = s["wnF"][...].reshape(fin, hid)
        s["wsT"][...] = dot(eye_w, w_self, 1, 1).astype(BF16)
        s["wnT"][...] = dot(eye_w, w_neigh, 1, 1).astype(BF16)
        x_full = s["xq"][...].reshape(fin, LANES)
        s["pre0"][...] = dot(s["wsT"][...], x_full, 1, 0) + s["biasF"][...].reshape(hid, LANES)
        far_all = pltpu.make_async_copy(s["A"], s["A"], far_sem)
        far_all.wait()

        def pass_on0(i):
            b0.arrive(i)
            c0.start(i + 1)

        def pass_on1(i):
            b1.arrive(i)
            c1.start(i + 1)

        each(ys - 1, pass_on0)
        each(zs - 1, pass_on1)
        c0.arrive_all()
        c1.arrive_all()

        iota = lax.broadcasted_iota(jnp.int32, (half, LANES), 0)
        zero = jnp.zeros((half, LANES), BF16)
        step = 4

        def place(f4):
            for k in range(step):
                f = f4 * step + k
                cols = pl.ds(pl.multiple_of(f * LANES, LANES), LANES)
                src = src_s[f]
                chip = src // CORES
                core = src - chip * CORES
                sy = chip // zs
                sz = chip - sy * zs
                lo = e0[core, chip]
                hi = e1[core, sz * ys + sy]
                row = row_s[f]
                for b in range(blks):
                    here = row == b
                    s["Lm"][b * cf : b * cf + half, cols] = lax.select(here, lo, zero)
                    s["Lm"][b * cf + half : (b + 1) * cf, cols] = lax.select(here, hi, zero)
                s["Lm"][blks * cf :, cols] = jnp.where(iota == row, 1.0, 0.0).astype(BF16)

        each(far // step, place)
        far_sum = dot(s["Lm"][...], s["A"][...], 1, 1)
        for b in range(blks):
            deg = s["near"][b, cf : cf + 8] + far_sum[blks * cf + b : blks * cf + b + 1]
            s["deg"][b] = deg
            summed = s["near"][b, :cf] + far_sum[b * cf : (b + 1) * cf]
            s["agg"][b] = (summed / deg[:1]).astype(BF16)
        agg = along_x("agg", lambda p: s["agg"].at[p], lambda q: s["aq"].at[q])
        agg.start_all()
        s["aq"][x] = s["agg"][x]
        deg_row = s["deg"][x][:1]
        agg.arrive_all()

        agg_full = s["aq"][...].reshape(fin, LANES)
        pre = s["pre0"][...] + dot(s["wnT"][...], agg_full, 1, 0)
        sigma = jax.nn.sigmoid(pre)
        cot = s["cq"][...].reshape(hid, LANES).astype(F32)
        grad_pre = cot * sigma * (1.0 + pre * (1.0 - sigma))
        grad_low = grad_pre.astype(BF16)
        neigh = dot(s["wnF"][...].reshape(fin, hid), grad_low, 1, 0)
        s["ss"][...] = (neigh / deg_row).astype(BF16).reshape(xs, cf, LANES)
        scaled = along_x("scaled", lambda p: s["ss"].at[p], lambda q: s["sq"].at[q])
        scaled.start_all()
        s["sq"][x] = s["ss"][x]

        pieces = (dot(x_full, grad_low, 1, 1), dot(agg_full, grad_low, 1, 1))
        bias_row = dot(jnp.ones((8, LANES), F32), grad_pre, 1, 1, lax.Precision.HIGHEST)
        rows8 = lax.broadcasted_iota(jnp.int32, (8, LANES), 0)
        bias_tile = jnp.zeros((8, LANES), F32)
        for l in range(lane_groups):
            bias_tile = jnp.where(rows8 == l, bias_row[:, l * LANES : (l + 1) * LANES], bias_tile)
        for q in range(xs):
            t = 0
            for piece in pieces:
                for r in range(cf // 8):
                    for l in range(lane_groups):
                        at = q * cf + r * 8
                        s["gx"][q, t] = piece[at : at + 8, l * LANES : (l + 1) * LANES]
                        t += 1
            s["gx"][q, tiles] = bias_tile
        gx = along_x("gx", lambda p: s["gx"].at[p], lambda q: s["gxr"].at[q])
        gx.start_all()
        s["gxr"][x] = s["gx"][x]
        s["st"][...] = dot(s["wsF"][...].reshape(fin, hid), grad_low, 1, 0).reshape(xs, cf, LANES)
        s["hs"][...] = (pre * sigma).astype(BF16).reshape(xs, ch, LANES)
        own_term = along_x("self", lambda p: s["st"].at[p], lambda q: s["stq"].at[q])
        hidden = along_x("hid", lambda p: s["hs"].at[p], lambda q: s["hq"].at[q])
        own_term.start_all()
        hidden.start_all()
        s["stq"][x] = s["st"][x]
        s["hq"][x] = s["hs"][x]

        scaled.arrive_all()

        def back(f4):
            for k in range(step):
                f = f4 * step + k
                cols = pl.ds(pl.multiple_of(f * LANES, LANES), LANES)
                s["BK"][f] = dot(s["sq"][row_s[f]], s["A"][:, cols], 1, 0)

        each(far // step, back)

        def slot(owner):
            f = inv_s[owner]
            return jnp.maximum(f, 0), (f >= 0).astype(F32)

        def share0(i):
            def one(k):
                at = i * zs + k
                f, there = slot(at * CORES + o)
                s["cs0"][at] = s["BK"][f, :half] * there

            for k in range(zs):
                one(k)
            core0.start(i)

        def share1(i):
            for k in range(ys):
                f, there = slot((k * zs + i) * CORES + o)
                s["cs1"][i * ys + k] = s["BK"][f, half:] * there
            core1.start(i)

        def of0(ref):
            return lambda i: ref.at[pl.ds(i * zs, zs)]

        def of1(ref):
            return lambda i: ref.at[pl.ds(i * ys, ys)]

        core0 = to_core("core0", of0(s["cs0"]), of0(s["cr0"]), of0(s["cr0"]))
        core1 = to_core("core1", of1(s["cs1"]), of1(s["cr1"]), of1(s["cr1"]))
        each(ys, share0)
        each(zs, share1)

        gx.arrive_all()
        for t in range(tiles + 1):
            total = s["gxr"][0, t]
            for q in range(1, xs):
                total = total + s["gxr"][q, t]
            if t < tiles:
                s["ga"][t // per, t % per] = total
            else:
                for g in range(groups):
                    s["ga"][g, per] = total
        ga = along_group("ga", lambda p: s["ga"].at[p], lambda q: s["gar"].at[q])
        ga.start_all()
        s["gar"][g_me] = s["ga"][g_me]

        spread = [None] * (blks + 2)
        for b in range(blks):
            for k in range(3):
                term = dot(s["sq"][b], s["band"][b, k], 1, 0)
                spread[b + k] = term if spread[b + k] is None else spread[b + k] + term
        s["ho"][0] = spread[0]
        s["ho"][1] = spread[blks + 1]
        for b in range(blks):
            s["inner"][b] = spread[b + 1]
        outward = to_sides("out", s["ho"].at[0], s["ho"].at[1], lambda i: s["hr"].at[i])
        outward.start_all()

        p0 = along_y("p0", lambda p: s["ps0"].at[pl.ds(p * zs, zs)], lambda q: s["pr0"].at[q], lambda q: s["pr0"].at[q])
        p1 = along_z("p1", lambda p: s["ps1"].at[pl.ds(p * ys, ys)], lambda q: s["pr1"].at[q], lambda q: s["pr1"].at[q])

        def add0(i):
            core0.arrive(i)
            for k in range(zs):
                at = i * zs + k
                f, there = slot(at * CORES + c)
                s["ps0"][at] = (s["BK"][f, :half] * there + s["cr0"][at]).astype(BF16)

        def add1(i):
            core1.arrive(i)
            for k in range(ys):
                at = i * ys + k
                f, there = slot((k * zs + i) * CORES + c)
                s["ps1"][at] = (s["BK"][f, half:] * there + s["cr1"][at]).astype(BF16)

        each(ys, add0)
        p0.start_all()
        each(zs, add1)
        p1.start_all()
        s["pr0"][y] = s["ps0"][pl.ds(y * zs, zs)]
        s["pr1"][z] = s["ps1"][pl.ds(z * ys, ys)]

        ga.arrive_all()
        total = s["gar"][0]
        for g in range(1, groups):
            total = total + s["gar"][g]
        s["gb"][...] = total
        gy = along_y("gy", lambda p: s["gb"], lambda q: s["gyr"].at[q], lambda q: s["gyr"].at[q])
        gy.start_all()
        s["gyr"][y] = total
        gy.arrive_all()
        total = s["gyr"][0]
        for q in range(1, ys):
            total = total + s["gyr"][q]
        s["gt"][...] = total[:per]
        gb_o[...] = total[per]
        gz = along_group("gz", lambda p: s["gt"], lambda q: s["gzr"].at[q])
        gz.start_all()
        s["gzr"][g_me] = total[:per]

        def add_up(ref, count):
            total = ref[0].astype(F32)
            for q in range(1, count):
                total = total + ref[q].astype(F32)
            return total

        p0.arrive_all()
        s["q0"][...] = add_up(s["pr0"], ys)
        r0 = along_z("r0", lambda p: s["q0"].at[p], lambda q: s["f0"].at[q], lambda q: s["f0"].at[q])
        r0.start_all()
        p1.arrive_all()
        s["q1"][...] = add_up(s["pr1"], zs)
        r1 = along_y("r1", lambda p: s["q1"].at[p], lambda q: s["f1"].at[q], lambda q: s["f1"].at[q])
        r1.start_all()
        s["f0"][z] = s["q0"][z]
        s["f1"][y] = s["q1"][y]

        own_term.arrive_all()
        hidden.arrive_all()
        hid_o[...] = s["hq"][...]
        outward.arrive_all()
        gz.arrive_all()
        gt_o[...] = s["gzr"][...].reshape(tiles, 8, LANES)
        r0.arrive_all()
        r1.arrive_all()
        far_total = jnp.concatenate([add_up(s["f0"], zs), add_up(s["f1"], ys)], 0)
        for b in range(blks):
            value = s["inner"][b]
            if b == 0:
                value = value + s["hr"][0]
            if b == blks - 1:
                value = value + s["hr"][1]
            value = s["stq"][b] + value
            value = value + lax.select(eb == b, far_total, jnp.zeros_like(far_total))
            gf_o[b] = value.astype(BF16)

        for one in (
            a0, a1, halo, *early, b0, b1, c0, c1, agg, scaled, gx, own_term, hidden, core0, core1, ga, outward,
            p0, p1, gy, gz, r0, r1,
        ):
            one.drain()

    outs = (
        jax.ShapeDtypeStruct((blks, ch, LANES), BF16),
        jax.ShapeDtypeStruct((blks, cf, LANES), BF16),
        jax.ShapeDtypeStruct((tiles, 8, LANES), F32),
        jax.ShapeDtypeStruct((8, LANES), F32),
    )
    scratch_shapes = [pltpu.VMEM(shape, dtype) for shape, dtype in scratch.values()] + [
        pltpu.SemaphoreType.DMA((n_sems,)),
        pltpu.SemaphoreType.DMA((n_sems,)),
        pltpu.SemaphoreType.DMA,
        pltpu.SemaphoreType.DMA,
    ]
    smem = pl.BlockSpec(memory_space=pltpu.SMEM)
    vmem = pl.BlockSpec(memory_space=pltpu.VMEM)
    hbm = pl.BlockSpec(memory_space=pl.ANY)
    call = pl.pallas_call(
        kernel,
        out_shape=outs,
        in_specs=[smem] * 4 + [vmem] * 5 + [hbm] * 2,
        out_specs=[vmem] * 4,
        scratch_shapes=scratch_shapes,
        compiler_params=pltpu.CompilerParams(
            collective_id=0, has_side_effects=True, vmem_limit_bytes=40 * 1024 * 1024
        ),
        name="layer",
    )

    def lay_out(hid_ref, gf_ref, gt_ref, gb_ref, hid_o, gf_o, gs_o, gn_o, gb_o):
        eye_n = eye(LANES, BF16)
        for b in range(blks):
            rows = slice(b * LANES, (b + 1) * LANES)
            hid_o[rows, :] = dot(eye_n, hid_ref[b], 1, 1).astype(BF16)
            gf_o[rows, :] = dot(eye_n, gf_ref[b], 1, 1).astype(BF16)
        t = 0
        for out in (gs_o, gn_o):
            for r in range(cf // 8):
                for l in range(lane_groups):
                    out[r * 8 : (r + 1) * 8, l * LANES : (l + 1) * LANES] = gt_ref[t]
                    t += 1
        x = lax.axis_index("feat")
        row = jnp.zeros((1, ch), F32)
        for q in range(xs):
            at = q * ch
            part = gb_ref[at // LANES : at // LANES + 1, at % LANES : at % LANES + ch]
            row = jnp.where(x == q, part, row)
        gb_o[...] = row

    finish = pl.pallas_call(
        lay_out,
        out_shape=(
            jax.ShapeDtypeStruct((blks * LANES, ch), BF16),
            jax.ShapeDtypeStruct((blks * LANES, cf), BF16),
            jax.ShapeDtypeStruct((cf, hid), F32),
            jax.ShapeDtypeStruct((cf, hid), F32),
            jax.ShapeDtypeStruct((1, ch), F32),
        ),
        in_specs=[vmem] * 4,
        out_specs=[vmem] * 5,
        name="lay_out",
    )
    return call, finish


def solution(mesh):
    nodes, xs = mesh.shape["nodes"], mesh.shape["feat"]
    ys, zs = sides(nodes)

    def on_device(
        features, band_counts, far_counts, far_row, far_src, export_block, w_self, w_neigh, bias, cotangent
    ):
        far = far_counts.shape[0]
        hid = w_self.shape[1]
        call, finish = make_kernel(ys, zs, xs, far, hid)
        match = far_src[None, :] == jnp.arange(nodes, dtype=jnp.int32)[:, None]
        inverse = jnp.max(jnp.where(match, jnp.arange(far, dtype=jnp.int32)[None, :], -1), axis=1)
        wide_bias = jnp.broadcast_to(bias[:, None], (bias.shape[0], LANES))
        parts = call(
            far_row, far_src, inverse, export_block, features, w_self, w_neigh, wide_bias, cotangent,
            band_counts, far_counts,
        )
        hidden, grad_features, grad_self, grad_neigh, grad_bias = finish(*parts)
        return hidden, grad_features, grad_self, grad_neigh, grad_bias.reshape(bias.shape)

    return jax.shard_map(
        on_device,
        mesh=mesh,
        in_specs=(
            P("nodes", "feat"),
            P("nodes", None, None, None),
            P("nodes", None, None),
            P("nodes"),
            P("nodes"),
            P("nodes"),
            P("feat", None),
            P("feat", None),
            P("feat"),
            P("nodes", "feat"),
        ),
        out_specs=(
            P("nodes", "feat"),
            P("nodes", "feat"),
            P("feat", None),
            P("feat", None),
            P("feat"),
        ),
        check_vma=False,
    )
```

time: 341 us -> 82.6 us (0.24)
  waiting for transfers between devices: 224 us -> 0 us
  Pallas kernels: 0 us -> 66.4 us
  blocking collectives: 47.1 us -> 0 us
  starting transfers between devices: 29.2 us -> 0 us
  between operations: 15 us -> 1.32 us
  matrix products: 9.55 us -> 0 us
  other arithmetic: 4.96 us -> 0.75 us
    psum x1 -> x0, waiting for transfers between devices: 157 us -> none  [on_device(): lax.psum((self_grad, neigh_grad, bias_part), 'nodes')]
    pallas_call x0 -> x2, Pallas kernels: none -> 66.4 us  [the longest x1 64.6 us: on_device(): call(far_row, far_src, inverse, export_block, features, w_self, w_neigh,...]
    all_gather x5 -> x0, blocking collectives: 47.1 us -> none  [the longest x1 9.85 us: on_device(): lax.all_gather(aggregate, 'feat', axis=1, tiled=True)]
    all_gather x1 -> x0, waiting for transfers between devices: 43.5 us -> none  [on_device(): exported = lax.all_gather(chosen, 'nodes', axis=0, tiled=True)]
    all_to_all x1 -> x0, waiting for transfers between devices: 20.9 us -> none  [on_device(): lax.all_to_all(slots.astype(jnp.bfloat16), 'nodes', split_axis=0, concat_...]
    ppermute x4 -> x0, starting transfers between devices: 15.6 us -> none  [the longest x2 8.14 us: padded_2(): lax.ppermute(tail, axis, [(i, (i + 1) % count) for i in range(ends)])]
    all_to_all x1 -> x0, starting transfers between devices: 13.5 us -> none  [on_device(): lax.all_to_all(slots.astype(jnp.bfloat16), 'nodes', split_axis=0, concat_...]
    dot_general x13 -> x0, matrix products: 9.55 us -> none  [the longest x1 1.71 us: on_device(): slots = jnp.einsum('fp,fjc->pjc', owner, far_back, precision=high)]
  transfers between devices with their start and end apart: 7 -> 0, of which waited for: 4 -> 0; matrix products, arithmetic and copies ran while one was open for 3% -> 0% of each run, Pallas kernels for 0% -> 0%
where the time goes in v1:
time: 82.6 us; the launch traced here: 82 us
  Pallas kernels  66.4 us (80%)
  local copies, waits for them, and re-layouts  13.6 us (16%)
  between operations  1.32 us (2%)
    pallas_call x1, Pallas kernels, on_device(): call(far_row, far_src, inverse, export_block, features, w_self, w_neigh,...  64.6 us
    unnamed x24, local copies, waits for them, and re-layouts  12.8 us
    pallas_call x1, Pallas kernels, on_device(): hidden, grad_features, grad_self, grad_neigh, grad_bias = finish(*parts)  1.81 us

profile of v1, /device:TPU:1, one launch (start us, length us, event | category | flops | bytes accessed | tf_op | source)
XLA Modules:
  0.0 82.0 jit_solution(12785641885431083986)
XLA Ops:
  1.3 0.7 select_reduce_fusion.inv_s
  2.0 0.7 broadcast_in_dim.23.bias_ref
  2.8 0.9 %copy.19.feat_ref = bf16[512,32]{1,0:T(8,128)(2,1)S(1)} copy(bf16[512,32]{0,1:T(8,128)(2,1)} %param.10) | data formatting | bytes 65536 | tf_op args[0]
  3.6 1.0 %copy.20.cot_ref = bf16[512,64]{1,0:T(8,128)(2,1)S(1)} copy(bf16[512,64]{0,1:T(8,128)(2,1)} %param.19) | data formatting | bytes 131072 | tf_op args[9]
  4.6 0.0 copy-start
  4.6 1.6 %copy-done = bf16[64,128,128]{2,1,0:T(8,128)(2,1)S(1)} copy-done((bf16[64,128,128]{2,1,0:T(8,128)(2,1)S(1)}, bf16[64,128,128]{2,1,0:T(8,128)(2,1)}, u32[]{:S(2)}) %copy-start) | copy-done | bytes 2097176
  6.2 0.0 copy-start.1
  6.2 1.0 %copy-done.1 = bf16[4,3,128,128]{3,2,1,0:T(8,128)(2,1)S(1)} copy-done((bf16[4,3,128,128]{3,2,1,0:T(8,128)(2,1)S(1)}, bf16[4,3,128,128]{3,2,1,0:T(8,128)(2,1)}, u32[]{:S(2)}) %copy-start.1) | copy-done | bytes 393240
  7.2 0.0 copy-start.5
  7.2 0.7 copy-done.5
  7.9 0.0 copy-start.6
  7.9 0.7 copy-done.6
  8.6 0.0 copy-start.8
  8.6 0.7 copy-done.8
  9.3 0.7 copy-done.9
  9.9 64.6 %layer.1 = (bf16[4,64,128]{2,1,0:T(8,128)(2,1)S(1)}, bf16[4,32,128]{2,1,0:T(8,128)(2,1)S(1)}, f32[16,8,128]{2,1,0:T(8,128)S(1)}, f32[8,128]{1,0:T(8,128)S(1)}) custom-call(s32[64]{0:T(128)S(1)} %copy-done.8, s32[64]{0:T(128)S(1)} %copy-done.9, s32[128]{0:T(128)S(1)} %select_reduce_fusion.inv_s, s32[1]{0:T(128)S(6)} %copy.23.eb_s, ...), custom_call_target="tpu_custom_call" | custom-call | tf_op jit(solution)/shard_map/layer/pallas_call | solution.py:637
  74.5 0.0 copy-start.2
  74.5 0.6 copy-done.2
  75.2 0.6 copy-done.3
  75.8 0.6 copy-done.4
  76.4 0.6 copy-done.7
  77.0 1.8 %lay_out.1 = (bf16[512,64]{1,0:T(8,128)(2,1)}, bf16[512,32]{1,0:T(8,128)(2,1)}, f32[32,256]{1,0:T(8,128)}, f32[32,256]{1,0:T(8,128)}, f32[1,64]{1,0:T(1,128)}) custom-call(bf16[4,64,128]{2,1,0:T(8,128)(2,1)} %copy-done.2, bf16[4,32,128]{2,1,0:T(8,128)(2,1)} %copy-done.4, f32[16,8,128]{2,1,0:T(8,128)} %copy-done.3, f32[8,128]{1,0:T(8,128)} %copy-done.7), custom_call_target="tpu_custom_call" | custom-call | tf_op jit(solution)/shard_map/lay_out/pallas_call | solution.py:641
  78.8 1.6 %copy.21 = bf16[512,64]{0,1:T(8,128)(2,1)} copy(bf16[512,64]{1,0:T(8,128)(2,1)} %get-tuple-element.28) | data formatting | bytes 131072
  80.4 1.6 %copy.22 = bf16[512,32]{0,1:T(8,128)(2,1)} copy(bf16[512,32]{1,0:T(8,128)(2,1)} %get-tuple-element.29) | data formatting | bytes 65536
  (4 shorter events, 0.0 us)
Async XLA Ops:
  4.6 1.6 %copy-start = (bf16[64,128,128]{2,1,0:T(8,128)(2,1)S(1)}, bf16[64,128,128]{2,1,0:T(8,128)(2,1)}, u32[]{:S(2)}) copy-start(bf16[64,128,128]{2,1,0:T(8,128)(2,1)} %far_hbm.1) | copy-start | bytes 6291460
  6.2 1.0 %copy-start.1 = (bf16[4,3,128,128]{3,2,1,0:T(8,128)(2,1)S(1)}, bf16[4,3,128,128]{3,2,1,0:T(8,128)(2,1)}, u32[]{:S(2)}) copy-start(bf16[4,3,128,128]{3,2,1,0:T(8,128)(2,1)} %band_hbm.1) | copy-start | bytes 1179652
  7.2 0.7 copy-start.5
  7.9 0.7 copy-start.6
  8.6 0.7 copy-start.8
  9.3 0.7 copy-start.9
  74.5 0.6 copy-start.2
  75.2 0.6 copy-start.3
  75.8 0.6 copy-start.4
  76.4 0.6 copy-start.7

commit v2 on v1

--- a/solution.py
+++ b/solution.py
@@ -10,6 +10,7 @@
 BF16 = jnp.bfloat16
 LANES = 128
 CORES = 2
+VMEM_LIMIT = 60 * 1024 * 1024
 
 
 def sides(nodes):
@@ -104,9 +105,10 @@
     n_sems = sum(c for _, c in sem_plan.values())
 
     scratch = dict(
+        feat=((cf, blks * LANES), BF16), cot=((ch, blks * LANES), BF16), inv=((1, nodes), jnp.int32),
         XT=((blks, cf, LANES), BF16), xq=((xs, cf, LANES), BF16),
         cT=((blks, ch, LANES), BF16), cq=((xs, ch, LANES), BF16),
-        wsF=((xs, cf, hid), BF16), wnF=((xs, cf, hid), BF16), biasF=((xs, ch, LANES), F32),
+        wsF=((xs, cf, hid), BF16), wnF=((xs, cf, hid), BF16), biasF=((xs, 8, LANES), F32),
         wsT=((hid, fin), BF16), wnT=((hid, fin), BF16), pre0=((hid, LANES), F32),
         e0=((CORES, chips, half, LANES), BF16), e1=((CORES, chips, half, LANES), BF16),
         halo=((2, cf, LANES), BF16),
@@ -134,11 +136,11 @@
     names = list(scratch)
 
     def kernel(
-        row_s, src_s, inv_s, eb_s, feat_ref, ws_ref, wn_ref, bias_ref, cot_ref, band_hbm, far_hbm,
-        hid_o, gf_o, gt_o, gb_o, *rest,
+        row_s, src_s, eb_s, bias_ref, src_ref, feat_hbm, cot_hbm, ws_hbm, wn_hbm, band_hbm, far_hbm,
+        hid_o, gf_o, gs_o, gn_o, gb_o, *rest,
     ):
         s = dict(zip(names, rest))
-        send_sems, recv_sems, far_sem, band_sem = rest[len(names):]
+        send_sems, recv_sems, local_sems, inv_s = rest[len(names):]
         n = lax.axis_index("nodes")
         x = lax.axis_index("feat")
         c = n % CORES
@@ -209,19 +211,13 @@
         def to_core(name, src, there, here):
             return stage(name, lambda i: (src(i), there(i), (node(y, z, o), x)), here)
 
-        def start_far(f):
-            cols = pl.ds(pl.multiple_of(f * LANES, LANES), LANES)
-            pltpu.make_async_copy(far_hbm.at[f], s["A"].at[:, cols], far_sem).start()
-
-        each(far, start_far)
-        band_copy = pltpu.make_async_copy(band_hbm, s["band"], band_sem)
-        band_copy.start()
-
         barrier = pltpu.get_barrier_semaphore()
 
         def greet(device):
             pl.semaphore_signal(barrier, inc=1, device_id=device, device_id_type=MESH)
 
+        feat_copy = pltpu.make_async_copy(feat_hbm, s["feat"], local_sems.at[0])
+        feat_copy.start()
         each(ys - 1, lambda i: greet((node((y + i + 1) % ys, z, c), x)))
 
         def greet_group(i):
@@ -232,19 +228,20 @@
         each(xs - 1, lambda i: greet((n, (x + i + 1) % xs)))
         greet((left, x))
         greet((right, x))
-
-        eye_f = eye(cf, BF16)
-        eye_h = eye(ch, BF16)
-        for b in range(blks):
-            rows = slice(b * LANES, (b + 1) * LANES)
-            s["XT"][b] = dot(eye_f, feat_ref[rows, :], 1, 1).astype(BF16)
+        cot_copy = pltpu.make_async_copy(cot_hbm, s["cot"], local_sems.at[1])
+        ws_copy = pltpu.make_async_copy(ws_hbm, s["wsF"].at[x], local_sems.at[2])
+        wn_copy = pltpu.make_async_copy(wn_hbm, s["wnF"].at[x], local_sems.at[3])
+        band_copy = pltpu.make_async_copy(band_hbm, s["band"], local_sems.at[4])
+        for one in (ws_copy, wn_copy, cot_copy, band_copy):
+            one.start()
+
+        feat_copy.wait()
+        for b in range(blks):
+            s["XT"][b] = s["feat"][:, b * LANES : (b + 1) * LANES]
         eb = eb_s[0]
         mine = s["XT"][eb]
         s["e0"][c, y * zs + z] = mine[:half]
         s["e1"][c, z * ys + y] = mine[half:]
-        for b in range(blks):
-            rows = slice(b * LANES, (b + 1) * LANES)
-            s["cT"][b] = dot(eye_h, cot_ref[rows, :], 1, 1).astype(BF16)
 
         pl.semaphore_wait(barrier, ys - 1 + groups - 1 + xs - 1 + 2)
 
@@ -256,18 +253,39 @@
         halo = to_sides("halo", s["XT"].at[0], s["XT"].at[blks - 1], lambda i: s["halo"].at[i])
         halo.start_all()
         xq = along_x("xq", lambda p: s["XT"].at[p], lambda q: s["xq"].at[q])
-        ws = along_x("ws", lambda p: ws_ref, lambda q: s["wsF"].at[q])
-        wn = along_x("wn", lambda p: wn_ref, lambda q: s["wnF"].at[q])
-        bias = along_x("bias", lambda p: bias_ref, lambda q: s["biasF"].at[q])
+        ws = along_x("ws", lambda p: s["wsF"].at[x], lambda q: s["wsF"].at[q])
+        wn = along_x("wn", lambda p: s["wnF"].at[x], lambda q: s["wnF"].at[q])
+        bias = along_x("bias", lambda p: s["biasF"].at[x], lambda q: s["biasF"].at[q])
         cq = along_x("cq", lambda p: s["cT"].at[p], lambda q: s["cq"].at[q])
         early = (xq, ws, wn, bias, cq)
-        for one in early:
-            one.start_all()
+        xq.start_all()
+        ws_copy.wait()
+        ws.start_all()
+        wn_copy.wait()
+        wn.start_all()
+        cot_copy.wait()
+        for b in range(blks):
+            s["cT"][b] = s["cot"][:, b * LANES : (b + 1) * LANES]
+        cq.start_all()
+        s["biasF"][x] = jnp.zeros((8, LANES), F32)
+        s["biasF"][x, 0:1, 0:ch] = bias_ref[...]
+        bias.start_all()
         s["xq"][x] = s["XT"][x]
         s["cq"][x] = s["cT"][x]
-        s["wsF"][x] = ws_ref[...]
-        s["wnF"][x] = wn_ref[...]
-        s["biasF"][x] = bias_ref[...]
+
+        def start_far(f):
+            cols = pl.ds(pl.multiple_of(f * LANES, LANES), LANES)
+            pltpu.make_async_copy(far_hbm.at[f], s["A"].at[:, cols], local_sems.at[5]).start()
+
+        each(far, start_far)
+
+        diagonal = lax.broadcasted_iota(jnp.int32, (far, far), 0) == lax.broadcasted_iota(jnp.int32, (far, far), 1)
+        src_col = jnp.max(jnp.where(diagonal, src_ref[...], 0), axis=1, keepdims=True)
+        owners = lax.broadcasted_iota(jnp.int32, (far, nodes), 1)
+        index = lax.broadcasted_iota(jnp.int32, (far, nodes), 0)
+        s["inv"][...] = jnp.max(jnp.where(src_col == owners, index, -1), axis=0, keepdims=True)
+        inv_copy = pltpu.make_async_copy(s["inv"], inv_s, local_sems.at[6])
+        inv_copy.start()
 
         def row0(q):
             return e0.at[c, pl.ds(q * zs, zs)]
@@ -316,9 +334,14 @@
         s["wsT"][...] = dot(eye_w, w_self, 1, 1).astype(BF16)
         s["wnT"][...] = dot(eye_w, w_neigh, 1, 1).astype(BF16)
         x_full = s["xq"][...].reshape(fin, LANES)
-        s["pre0"][...] = dot(s["wsT"][...], x_full, 1, 0) + s["biasF"][...].reshape(hid, LANES)
-        far_all = pltpu.make_async_copy(s["A"], s["A"], far_sem)
+        own_part = dot(s["wsT"][...], x_full, 1, 0)
+        eye_h = eye(ch, F32)
+        for q in range(xs):
+            bias_col = jnp.sum(s["biasF"][q, 0:1, 0:ch] * eye_h, axis=1, keepdims=True)
+            s["pre0"][q * ch : (q + 1) * ch] = own_part[q * ch : (q + 1) * ch] + bias_col
+        far_all = pltpu.make_async_copy(s["A"], s["A"], local_sems.at[5])
         far_all.wait()
+        inv_copy.wait()
 
         def pass_on0(i):
             b0.arrive(i)
@@ -418,8 +441,8 @@
         each(far // step, back)
 
         def slot(owner):
-            f = inv_s[owner]
-            return jnp.maximum(f, 0), (f >= 0).astype(F32)
+            f = inv_s[0, owner]
+            return jnp.minimum(jnp.maximum(f, 0), far - 1), (f >= 0).astype(F32)
 
         def share0(i):
             def one(k):
@@ -511,7 +534,12 @@
         for q in range(1, ys):
             total = total + s["gyr"][q]
         s["gt"][...] = total[:per]
-        gb_o[...] = total[per]
+        gb_row = jnp.zeros((1, ch), F32)
+        for q in range(xs):
+            at = q * ch
+            part = total[per, at // LANES : at // LANES + 1, at % LANES : at % LANES + ch]
+            gb_row = jnp.where(x == q, part, gb_row)
+        gb_o[...] = gb_row
         gz = along_group("gz", lambda p: s["gt"], lambda q: s["gzr"].at[q])
         gz.start_all()
         s["gzr"][g_me] = total[:per]
@@ -535,10 +563,16 @@
 
         own_term.arrive_all()
         hidden.arrive_all()
-        hid_o[...] = s["hq"][...]
+        for b in range(blks):
+            hid_o[:, b * LANES : (b + 1) * LANES] = s["hq"][b]
         outward.arrive_all()
         gz.arrive_all()
-        gt_o[...] = s["gzr"][...].reshape(tiles, 8, LANES)
+        t = 0
+        for out in (gs_o, gn_o):
+            for r in range(cf // 8):
+                for l in range(lane_groups):
+                    out[r * 8 : (r + 1) * 8, l * LANES : (l + 1) * LANES] = s["gzr"][t // per, t % per]
+                    t += 1
         r0.arrive_all()
         r1.arrive_all()
         far_total = jnp.concatenate([add_up(s["f0"], zs), add_up(s["f1"], ys)], 0)
@@ -550,7 +584,7 @@
                 value = value + s["hr"][1]
             value = s["stq"][b] + value
             value = value + lax.select(eb == b, far_total, jnp.zeros_like(far_total))
-            gf_o[b] = value.astype(BF16)
+            gf_o[:, b * LANES : (b + 1) * LANES] = value.astype(BF16)
 
         for one in (
             a0, a1, halo, *early, b0, b1, c0, c1, agg, scaled, gx, own_term, hidden, core0, core1, ga, outward,
@@ -559,16 +593,17 @@
             one.drain()
 
     outs = (
-        jax.ShapeDtypeStruct((blks, ch, LANES), BF16),
-        jax.ShapeDtypeStruct((blks, cf, LANES), BF16),
-        jax.ShapeDtypeStruct((tiles, 8, LANES), F32),
-        jax.ShapeDtypeStruct((8, LANES), F32),
+        jax.ShapeDtypeStruct((ch, blks * LANES), BF16),
+        jax.ShapeDtypeStruct((cf, blks * LANES), BF16),
+        jax.ShapeDtypeStruct((cf, hid), F32),
+        jax.ShapeDtypeStruct((cf, hid), F32),
+        jax.ShapeDtypeStruct((1, ch), F32),
     )
     scratch_shapes = [pltpu.VMEM(shape, dtype) for shape, dtype in scratch.values()] + [
         pltpu.SemaphoreType.DMA((n_sems,)),
         pltpu.SemaphoreType.DMA((n_sems,)),
-        pltpu.SemaphoreType.DMA,
-        pltpu.SemaphoreType.DMA,
+        pltpu.SemaphoreType.DMA((7,)),
+        pltpu.SMEM((1, nodes), jnp.int32),
     ]
     smem = pl.BlockSpec(memory_space=pltpu.SMEM)
     vmem = pl.BlockSpec(memory_space=pltpu.VMEM)
@@ -576,47 +611,31 @@
     call = pl.pallas_call(
         kernel,
         out_shape=outs,
-        in_specs=[smem] * 4 + [vmem] * 5 + [hbm] * 2,
-        out_specs=[vmem] * 4,
+        in_specs=[smem] * 3 + [vmem] * 2 + [hbm] * 6,
+        out_specs=[vmem] * 5,
         scratch_shapes=scratch_shapes,
         compiler_params=pltpu.CompilerParams(
-            collective_id=0, has_side_effects=True, vmem_limit_bytes=40 * 1024 * 1024
+            collective_id=0, has_side_effects=True, vmem_limit_bytes=VMEM_LIMIT
         ),
         name="layer",
     )
 
-    def lay_out(hid_ref, gf_ref, gt_ref, gb_ref, hid_o, gf_o, gs_o, gn_o, gb_o):
-        eye_n = eye(LANES, BF16)
-        for b in range(blks):
-            rows = slice(b * LANES, (b + 1) * LANES)
-            hid_o[rows, :] = dot(eye_n, hid_ref[b], 1, 1).astype(BF16)
-            gf_o[rows, :] = dot(eye_n, gf_ref[b], 1, 1).astype(BF16)
-        t = 0
-        for out in (gs_o, gn_o):
-            for r in range(cf // 8):
-                for l in range(lane_groups):
-                    out[r * 8 : (r + 1) * 8, l * LANES : (l + 1) * LANES] = gt_ref[t]
-                    t += 1
-        x = lax.axis_index("feat")
-        row = jnp.zeros((1, ch), F32)
-        for q in range(xs):
-            at = q * ch
-            part = gb_ref[at // LANES : at // LANES + 1, at % LANES : at % LANES + ch]
-            row = jnp.where(x == q, part, row)
-        gb_o[...] = row
+    def pass_through(*refs):
+        sems = refs[-1]
+        copies = [pltpu.make_async_copy(refs[i], refs[i + 5], sems.at[i]) for i in range(5)]
+        for one in copies:
+            one.start()
+        for one in copies:
+            one.wait()
 
     finish = pl.pallas_call(
-        lay_out,
-        out_shape=(
-            jax.ShapeDtypeStruct((blks * LANES, ch), BF16),
-            jax.ShapeDtypeStruct((blks * LANES, cf), BF16),
-            jax.ShapeDtypeStruct((cf, hid), F32),
-            jax.ShapeDtypeStruct((cf, hid), F32),
-            jax.ShapeDtypeStruct((1, ch), F32),
-        ),
-        in_specs=[vmem] * 4,
-        out_specs=[vmem] * 5,
-        name="lay_out",
+        pass_through,
+        out_shape=outs,
+        in_specs=[hbm] * 5,
+        out_specs=[hbm] * 5,
+        scratch_shapes=[pltpu.SemaphoreType.DMA((5,))],
+        compiler_params=pltpu.CompilerParams(vmem_limit_bytes=VMEM_LIMIT),
+        name="pass_through",
     )
     return call, finish
 
@@ -631,15 +650,12 @@
         far = far_counts.shape[0]
         hid = w_self.shape[1]
         call, finish = make_kernel(ys, zs, xs, far, hid)
-        match = far_src[None, :] == jnp.arange(nodes, dtype=jnp.int32)[:, None]
-        inverse = jnp.max(jnp.where(match, jnp.arange(far, dtype=jnp.int32)[None, :], -1), axis=1)
-        wide_bias = jnp.broadcast_to(bias[:, None], (bias.shape[0], LANES))
         parts = call(
-            far_row, far_src, inverse, export_block, features, w_self, w_neigh, wide_bias, cotangent,
-            band_counts, far_counts,
+            far_row, far_src, export_block, bias.reshape(1, -1), far_src.reshape(1, -1), features.T, cotangent.T,
+            w_self, w_neigh, band_counts, far_counts,
         )
         hidden, grad_features, grad_self, grad_neigh, grad_bias = finish(*parts)
-        return hidden, grad_features, grad_self, grad_neigh, grad_bias.reshape(bias.shape)
+        return hidden.T, grad_features.T, grad_self, grad_neigh, grad_bias.reshape(bias.shape)
 
     return jax.shard_map(
         on_device,

time: 82.6 us -> 72.2 us (0.87)
  local copies, waits for them, and re-layouts: 13.6 us -> 0 us
  Pallas kernels: 66.4 us -> 70.7 us
    unnamed x24 -> x0, local copies, waits for them, and re-layouts: 12.8 us -> none
    pallas_call x1, Pallas kernels: 1.81 us -> 6.13 us  [on_device(): hidden, grad_features, grad_self, grad_neigh, grad_bias = finish(*parts)]
where the time goes in v2:
time: 72.2 us; the launch traced here: 72 us
  Pallas kernels  70.7 us (98%)
  between operations  1.29 us (2%)
    pallas_call x1, Pallas kernels, on_device(): call(far_row, far_src, export_block, bias.reshape(1, -1), far_src.reshape...  64.6 us
    pallas_call x1, Pallas kernels, on_device(): hidden, grad_features, grad_self, grad_neigh, grad_bias = finish(*parts)  6.13 us

profile of v2, /device:TPU:1, one launch (start us, length us, event | category | flops | bytes accessed | tf_op | source)
XLA Modules:
  0.0 72.0 jit_solution(18212315060154040523)
XLA Ops:
  1.3 64.6 %layer.1 = (bf16[64,512]{1,0:T(8,128)(2,1)}, bf16[32,512]{1,0:T(8,128)(2,1)}, f32[32,256]{1,0:T(8,128)}, f32[32,256]{1,0:T(8,128)}, f32[1,64]{1,0:T(1,128)}) custom-call(s32[64]{0:T(128)} %row_s.1, s32[64]{0:T(128)} %src_s.1, s32[1]{0:T(128)S(6)} %copy.15.eb_s, f32[1,64]{1,0:T(1,128)} %bitcast.10, s32[1,64]{1,0:T(1,128)} %bitcast.9, ...), custom_call_target="tpu_custom_call" | custom-call | tf_op jit(solution)/shard_map/layer/pallas_call | solution.py:653
  65.9 6.1 %pass_through.1 = (bf16[64,512]{1,0:T(8,128)(2,1)}, bf16[32,512]{1,0:T(8,128)(2,1)}, f32[32,256]{1,0:T(8,128)}, f32[32,256]{1,0:T(8,128)}, f32[1,64]{1,0:T(1,128)}) custom-call(bf16[64,512]{1,0:T(8,128)(2,1)} %get-tuple-element.15.refs_0_, bf16[32,512]{1,0:T(8,128)(2,1)} %get-tuple-element.16.refs_1_, f32[32,256]{1,0:T(8,128)} %get-tuple-element.17.refs_2_, ...), custom_call_target="tpu_custom_call" | custom-call | tf_op jit(solution)/shard_map/pass_through/pallas_call | solution.py:657

commit v3 on v2

--- a/solution.py
+++ b/solution.py
@@ -40,8 +40,8 @@
 
 
 def nearest(i, size):
-    k = i // 2 + 1
-    return k + (i % 2) * (size - 2 * k)
+    k = lax.div(i, 2) + 1
+    return k + lax.rem(i, 2) * (size - 2 * k)
 
 
 class Stage:
@@ -106,6 +106,9 @@
 
     scratch = dict(
         feat=((cf, blks * LANES), BF16), cot=((ch, blks * LANES), BF16), inv=((1, nodes), jnp.int32),
+        srcs=((1, far), jnp.int32), bias_row=((1, ch), F32),
+        hid_v=((ch, blks * LANES), BF16), gf_v=((cf, blks * LANES), BF16),
+        gs_v=((cf, hid), F32), gn_v=((cf, hid), F32), gb_v=((1, ch), F32),
         XT=((blks, cf, LANES), BF16), xq=((xs, cf, LANES), BF16),
         cT=((blks, ch, LANES), BF16), cq=((xs, ch, LANES), BF16),
         wsF=((xs, cf, hid), BF16), wnF=((xs, cf, hid), BF16), biasF=((xs, 8, LANES), F32),
@@ -136,16 +139,17 @@
     names = list(scratch)
 
     def kernel(
-        row_s, src_s, eb_s, bias_ref, src_ref, feat_hbm, cot_hbm, ws_hbm, wn_hbm, band_hbm, far_hbm,
-        hid_o, gf_o, gs_o, gn_o, gb_o, *rest,
+        row_hbm, src_hbm, eb_hbm, bias_hbm, srcs_hbm, feat_hbm, cot_hbm, ws_hbm, wn_hbm, band_hbm, far_hbm,
+        hid_hbm, gf_hbm, gs_hbm, gn_hbm, gb_hbm, *rest,
     ):
         s = dict(zip(names, rest))
-        send_sems, recv_sems, local_sems, inv_s = rest[len(names):]
+        send_sems, recv_sems, local_sems, inv_s, row_s, src_s, eb_s = rest[len(names):]
+        hid_o, gf_o, gs_o, gn_o, gb_o = (s[name] for name in ("hid_v", "gf_v", "gs_v", "gn_v", "gb_v"))
         n = lax.axis_index("nodes")
         x = lax.axis_index("feat")
-        c = n % CORES
-        z = (n // CORES) % zs
-        y = n // (CORES * zs)
+        c = lax.rem(n, CORES)
+        z = lax.rem(lax.div(n, CORES), zs)
+        y = lax.div(n, CORES * zs)
         o = 1 - c
         g_me = z * CORES + c
 
@@ -156,37 +160,41 @@
             base, count = sem_plan[name]
             return Stage(send_sems, recv_sems, base, count, to, landing)
 
-        def along_z(name, src, there, here):
+        def offset(i, size, far_first):
+            return nearest(size - 2 - i if far_first else i, size)
+
+        def along_z(name, src, there, here, far_first=False):
             def to(i):
-                d = nearest(i, zs)
-                peer = (z + d) % zs
+                peer = lax.rem(z + offset(i, zs, far_first), zs)
                 return src(peer), there(z), (node(y, peer, c), x)
 
-            return stage(name, to, lambda i: here((z - nearest(i, zs) + zs) % zs))
-
-        def along_y(name, src, there, here):
+            return stage(name, to, lambda i: here(lax.rem(z - offset(i, zs, far_first) + zs, zs)))
+
+        def along_y(name, src, there, here, far_first=False):
             def to(i):
-                d = nearest(i, ys)
-                peer = (y + d) % ys
+                peer = lax.rem(y + offset(i, ys, far_first), ys)
                 return src(peer), there(y), (node(peer, z, c), x)
 
-            return stage(name, to, lambda i: here((y - nearest(i, ys) + ys) % ys))
+            return stage(name, to, lambda i: here(lax.rem(y - offset(i, ys, far_first) + ys, ys)))
+
+        def across(i, size):
+            return 1 + lax.rem(i + size // 2 - 1, size - 1)
 
         def along_x(name, src, land):
             def to(i):
-                peer = (x + i + 1) % xs
+                peer = lax.rem(x + across(i, xs), xs)
                 return src(peer), land(x), (n, peer)
 
-            return stage(name, to, lambda i: land((x - i - 1 + xs) % xs))
+            return stage(name, to, lambda i: land(lax.rem(x - across(i, xs) + xs, xs)))
 
         def along_group(name, src, land):
             def to(i):
-                peer = (g_me + i + 1) % groups
-                return src(peer), land(g_me), (node(y, peer // CORES, peer % CORES), x)
-
-            return stage(name, to, lambda i: land((g_me - i - 1 + groups) % groups))
-
-        left, right = (n + nodes - 1) % nodes, (n + 1) % nodes
+                peer = lax.rem(g_me + across(i, groups), groups)
+                return src(peer), land(g_me), (node(y, lax.div(peer, CORES), lax.rem(peer, CORES)), x)
+
+            return stage(name, to, lambda i: land(lax.rem(g_me - across(i, groups) + groups, groups)))
+
+        left, right = lax.rem(n + nodes - 1, nodes), lax.rem(n + 1, nodes)
 
         def to_sides(name, first, last, land):
             def to(i):
@@ -216,28 +224,35 @@
         def greet(device):
             pl.semaphore_signal(barrier, inc=1, device_id=device, device_id_type=MESH)
 
-        feat_copy = pltpu.make_async_copy(feat_hbm, s["feat"], local_sems.at[0])
-        feat_copy.start()
-        each(ys - 1, lambda i: greet((node((y + i + 1) % ys, z, c), x)))
-
         def greet_group(i):
-            peer = (g_me + i + 1) % groups
-            greet((node(y, peer // CORES, peer % CORES), x))
-
+            peer = lax.rem(g_me + across(i, groups), groups)
+            greet((node(y, lax.div(peer, CORES), lax.rem(peer, CORES)), x))
+
+        def fetch(src, dst, sem):
+            one = pltpu.make_async_copy(src, dst, local_sems.at[sem])
+            one.start()
+            return one
+
+        each(ys - 1, lambda i: greet((node(lax.rem(y + offset(i, ys, True), ys), z, c), x)))
+        feat_copy = fetch(feat_hbm, s["feat"], 0)
+        eb_copy = fetch(eb_hbm, eb_s, 7)
         each(groups - 1, greet_group)
-        each(xs - 1, lambda i: greet((n, (x + i + 1) % xs)))
+        each(xs - 1, lambda i: greet((n, lax.rem(x + i + 1, xs))))
         greet((left, x))
         greet((right, x))
-        cot_copy = pltpu.make_async_copy(cot_hbm, s["cot"], local_sems.at[1])
-        ws_copy = pltpu.make_async_copy(ws_hbm, s["wsF"].at[x], local_sems.at[2])
-        wn_copy = pltpu.make_async_copy(wn_hbm, s["wnF"].at[x], local_sems.at[3])
-        band_copy = pltpu.make_async_copy(band_hbm, s["band"], local_sems.at[4])
-        for one in (ws_copy, wn_copy, cot_copy, band_copy):
-            one.start()
+        ws_copy = fetch(ws_hbm, s["wsF"].at[x], 2)
+        wn_copy = fetch(wn_hbm, s["wnF"].at[x], 3)
+        cot_copy = fetch(cot_hbm, s["cot"], 1)
+        bias_copy = fetch(bias_hbm, s["bias_row"], 8)
+        srcs_copy = fetch(srcs_hbm, s["srcs"], 9)
+        band_copy = fetch(band_hbm, s["band"], 4)
+        row_copy = fetch(row_hbm, row_s, 10)
+        src_copy = fetch(src_hbm, src_s, 11)
 
         feat_copy.wait()
         for b in range(blks):
             s["XT"][b] = s["feat"][:, b * LANES : (b + 1) * LANES]
+        eb_copy.wait()
         eb = eb_s[0]
         mine = s["XT"][eb]
         s["e0"][c, y * zs + z] = mine[:half]
@@ -246,8 +261,8 @@
         pl.semaphore_wait(barrier, ys - 1 + groups - 1 + xs - 1 + 2)
 
         e0, e1 = s["e0"], s["e1"]
-        a0 = along_z("a0", lambda p: e0.at[c, y * zs + z], lambda q: e0.at[c, y * zs + q], lambda q: e0.at[c, y * zs + q])
-        a1 = along_y("a1", lambda p: e1.at[c, z * ys + y], lambda q: e1.at[c, z * ys + q], lambda q: e1.at[c, z * ys + q])
+        a0 = along_z("a0", lambda p: e0.at[c, y * zs + z], *[lambda q: e0.at[c, y * zs + q]] * 2, far_first=True)
+        a1 = along_y("a1", lambda p: e1.at[c, z * ys + y], *[lambda q: e1.at[c, z * ys + q]] * 2, far_first=True)
         a0.start_all()
         a1.start_all()
         halo = to_sides("halo", s["XT"].at[0], s["XT"].at[blks - 1], lambda i: s["halo"].at[i])
@@ -268,7 +283,8 @@
             s["cT"][b] = s["cot"][:, b * LANES : (b + 1) * LANES]
         cq.start_all()
         s["biasF"][x] = jnp.zeros((8, LANES), F32)
-        s["biasF"][x, 0:1, 0:ch] = bias_ref[...]
+        bias_copy.wait()
+        s["biasF"][x, 0:1, 0:ch] = s["bias_row"][...]
         bias.start_all()
         s["xq"][x] = s["XT"][x]
         s["cq"][x] = s["cT"][x]
@@ -279,8 +295,9 @@
 
         each(far, start_far)
 
+        srcs_copy.wait()
         diagonal = lax.broadcasted_iota(jnp.int32, (far, far), 0) == lax.broadcasted_iota(jnp.int32, (far, far), 1)
-        src_col = jnp.max(jnp.where(diagonal, src_ref[...], 0), axis=1, keepdims=True)
+        src_col = jnp.max(jnp.where(diagonal, s["srcs"][...], 0), axis=1, keepdims=True)
         owners = lax.broadcasted_iota(jnp.int32, (far, nodes), 1)
         index = lax.broadcasted_iota(jnp.int32, (far, nodes), 0)
         s["inv"][...] = jnp.max(jnp.where(src_col == owners, index, -1), axis=0, keepdims=True)
@@ -297,10 +314,12 @@
         b1 = along_z("b1", lambda p: row1(z), row1, row1)
 
         def near_y(i):
-            return (y - nearest(i - 1, ys) * jnp.minimum(i, 1) + ys) % ys
+            i = jnp.int32(i)
+            return lax.rem(y - nearest(jnp.maximum(i - 1, 0), ys) * jnp.minimum(i, 1) + ys, ys)
 
         def near_z(i):
-            return (z - nearest(i - 1, zs) * jnp.minimum(i, 1) + zs) % zs
+            i = jnp.int32(i)
+            return lax.rem(z - nearest(jnp.maximum(i - 1, 0), zs) * jnp.minimum(i, 1) + zs, zs)
 
         c0 = to_core(
             "c0", lambda i: row0(near_y(i)), lambda i: row0(near_y(i)), lambda i: e0.at[o, pl.ds(near_y(i) * zs, zs)]
@@ -342,6 +361,8 @@
         far_all = pltpu.make_async_copy(s["A"], s["A"], local_sems.at[5])
         far_all.wait()
         inv_copy.wait()
+        row_copy.wait()
+        src_copy.wait()
 
         def pass_on0(i):
             b0.arrive(i)
@@ -358,16 +379,16 @@
 
         iota = lax.broadcasted_iota(jnp.int32, (half, LANES), 0)
         zero = jnp.zeros((half, LANES), BF16)
-        step = 4
+        step = min(8, far)
 
         def place(f4):
             for k in range(step):
                 f = f4 * step + k
                 cols = pl.ds(pl.multiple_of(f * LANES, LANES), LANES)
                 src = src_s[f]
-                chip = src // CORES
+                chip = lax.div(src, CORES)
                 core = src - chip * CORES
-                sy = chip // zs
+                sy = lax.div(chip, zs)
                 sz = chip - sy * zs
                 lo = e0[core, chip]
                 hi = e1[core, sz * ys + sy]
@@ -425,20 +446,21 @@
         s["hs"][...] = (pre * sigma).astype(BF16).reshape(xs, ch, LANES)
         own_term = along_x("self", lambda p: s["st"].at[p], lambda q: s["stq"].at[q])
         hidden = along_x("hid", lambda p: s["hs"].at[p], lambda q: s["hq"].at[q])
-        own_term.start_all()
-        hidden.start_all()
         s["stq"][x] = s["st"][x]
         s["hq"][x] = s["hs"][x]
 
         scaled.arrive_all()
 
-        def back(f4):
-            for k in range(step):
-                f = f4 * step + k
+        wide = min(16, far)
+
+        def back(f16):
+            for k in range(wide):
+                f = f16 * wide + k
                 cols = pl.ds(pl.multiple_of(f * LANES, LANES), LANES)
                 s["BK"][f] = dot(s["sq"][row_s[f]], s["A"][:, cols], 1, 0)
 
-        each(far // step, back)
+        each(far // wide, back)
+
 
         def slot(owner):
             f = inv_s[0, owner]
@@ -521,14 +543,33 @@
         s["pr0"][y] = s["ps0"][pl.ds(y * zs, zs)]
         s["pr1"][z] = s["ps1"][pl.ds(z * ys, ys)]
 
+        own_term.start_all()
+        hidden.start_all()
         ga.arrive_all()
         total = s["gar"][0]
         for g in range(1, groups):
             total = total + s["gar"][g]
         s["gb"][...] = total
-        gy = along_y("gy", lambda p: s["gb"], lambda q: s["gyr"].at[q], lambda q: s["gyr"].at[q])
+        gy = along_y("gy", lambda p: s["gb"], *[lambda q: s["gyr"].at[q]] * 2, far_first=True)
         gy.start_all()
         s["gyr"][y] = total
+        def add_up(ref, count):
+            total = ref[0].astype(F32)
+            for q in range(1, count):
+                total = total + ref[q].astype(F32)
+            return total
+
+        p0.arrive_all()
+        s["q0"][...] = add_up(s["pr0"], ys)
+        r0 = along_z("r0", lambda p: s["q0"].at[p], *[lambda q: s["f0"].at[q]] * 2, far_first=True)
+        r0.start_all()
+        p1.arrive_all()
+        s["q1"][...] = add_up(s["pr1"], zs)
+        r1 = along_y("r1", lambda p: s["q1"].at[p], *[lambda q: s["f1"].at[q]] * 2, far_first=True)
+        r1.start_all()
+        s["f0"][z] = s["q0"][z]
+        s["f1"][y] = s["q1"][y]
+
         gy.arrive_all()
         total = s["gyr"][0]
         for q in range(1, ys):
@@ -544,27 +585,11 @@
         gz.start_all()
         s["gzr"][g_me] = total[:per]
 
-        def add_up(ref, count):
-            total = ref[0].astype(F32)
-            for q in range(1, count):
-                total = total + ref[q].astype(F32)
-            return total
-
-        p0.arrive_all()
-        s["q0"][...] = add_up(s["pr0"], ys)
-        r0 = along_z("r0", lambda p: s["q0"].at[p], lambda q: s["f0"].at[q], lambda q: s["f0"].at[q])
-        r0.start_all()
-        p1.arrive_all()
-        s["q1"][...] = add_up(s["pr1"], zs)
-        r1 = along_y("r1", lambda p: s["q1"].at[p], lambda q: s["f1"].at[q], lambda q: s["f1"].at[q])
-        r1.start_all()
-        s["f0"][z] = s["q0"][z]
-        s["f1"][y] = s["q1"][y]
-
         own_term.arrive_all()
         hidden.arrive_all()
         for b in range(blks):
             hid_o[:, b * LANES : (b + 1) * LANES] = s["hq"][b]
+        hid_out = fetch(hid_o, hid_hbm, 12)
         outward.arrive_all()
         gz.arrive_all()
         t = 0
@@ -573,6 +598,9 @@
                 for l in range(lane_groups):
                     out[r * 8 : (r + 1) * 8, l * LANES : (l + 1) * LANES] = s["gzr"][t // per, t % per]
                     t += 1
+        gs_out = fetch(gs_o, gs_hbm, 13)
+        gn_out = fetch(gn_o, gn_hbm, 14)
+        gb_out = fetch(gb_o, gb_hbm, 15)
         r0.arrive_all()
         r1.arrive_all()
         far_total = jnp.concatenate([add_up(s["f0"], zs), add_up(s["f1"], ys)], 0)
@@ -585,12 +613,15 @@
             value = s["stq"][b] + value
             value = value + lax.select(eb == b, far_total, jnp.zeros_like(far_total))
             gf_o[:, b * LANES : (b + 1) * LANES] = value.astype(BF16)
+        gf_out = fetch(gf_o, gf_hbm, 16)
 
         for one in (
             a0, a1, halo, *early, b0, b1, c0, c1, agg, scaled, gx, own_term, hidden, core0, core1, ga, outward,
             p0, p1, gy, gz, r0, r1,
         ):
             one.drain()
+        for one in (hid_out, gs_out, gn_out, gb_out, gf_out):
+            one.wait()
 
     outs = (
         jax.ShapeDtypeStruct((ch, blks * LANES), BF16),
@@ -602,17 +633,19 @@
     scratch_shapes = [pltpu.VMEM(shape, dtype) for shape, dtype in scratch.values()] + [
         pltpu.SemaphoreType.DMA((n_sems,)),
         pltpu.SemaphoreType.DMA((n_sems,)),
-        pltpu.SemaphoreType.DMA((7,)),
+        pltpu.SemaphoreType.DMA((17,)),
         pltpu.SMEM((1, nodes), jnp.int32),
+        pltpu.SMEM((far,), jnp.int32),
+        pltpu.SMEM((far,), jnp.int32),
+        pltpu.SMEM((1,), jnp.int32),
     ]
-    smem = pl.BlockSpec(memory_space=pltpu.SMEM)
     vmem = pl.BlockSpec(memory_space=pltpu.VMEM)
     hbm = pl.BlockSpec(memory_space=pl.ANY)
     call = pl.pallas_call(
         kernel,
         out_shape=outs,
-        in_specs=[smem] * 3 + [vmem] * 2 + [hbm] * 6,
-        out_specs=[vmem] * 5,
+        in_specs=[hbm] * 11,
+        out_specs=[hbm] * 5,
         scratch_shapes=scratch_shapes,
         compiler_params=pltpu.CompilerParams(
             collective_id=0, has_side_effects=True, vmem_limit_bytes=VMEM_LIMIT
@@ -621,19 +654,14 @@
     )
 
     def pass_through(*refs):
-        sems = refs[-1]
-        copies = [pltpu.make_async_copy(refs[i], refs[i + 5], sems.at[i]) for i in range(5)]
-        for one in copies:
-            one.start()
-        for one in copies:
-            one.wait()
+        for i in range(5):
+            refs[i + 5][...] = refs[i][...]
 
     finish = pl.pallas_call(
         pass_through,
         out_shape=outs,
-        in_specs=[hbm] * 5,
-        out_specs=[hbm] * 5,
-        scratch_shapes=[pltpu.SemaphoreType.DMA((5,))],
+        in_specs=[vmem] * 5,
+        out_specs=[vmem] * 5,
         compiler_params=pltpu.CompilerParams(vmem_limit_bytes=VMEM_LIMIT),
         name="pass_through",
     )

time: 72.2 us -> 66.4 us (0.920)
  Pallas kernels: 70.7 us -> 64.9 us
    pallas_call x1, Pallas kernels: 6.13 us -> 1.55 us  [on_device(): hidden, grad_features, grad_self, grad_neigh, grad_bias = finish(*parts)]
    pallas_call x1, Pallas kernels: 64.6 us -> 63.4 us  [on_device(): call(far_row, far_src, export_block, bias.reshape(1, -1), far_src.reshape...]
where the time goes in v3:
time: 66.4 us; the launch traced here: 66.2 us
  Pallas kernels  64.9 us (98%)
  between operations  1.29 us (2%)
    pallas_call x1, Pallas kernels, on_device(): call(far_row, far_src, export_block, bias.reshape(1, -1), far_src.reshape...  63.4 us
    pallas_call x1, Pallas kernels, on_device(): hidden, grad_features, grad_self, grad_neigh, grad_bias = finish(*parts)  1.55 us

profile of v3, /device:TPU:1, one launch (start us, length us, event | category | flops | bytes accessed | tf_op | source)
XLA Modules:
  0.0 66.2 jit_solution(1215858126683008404)
XLA Ops:
  1.3 63.4 %layer.1 = (bf16[64,512]{1,0:T(8,128)(2,1)}, bf16[32,512]{1,0:T(8,128)(2,1)}, f32[32,256]{1,0:T(8,128)}, f32[32,256]{1,0:T(8,128)}, f32[1,64]{1,0:T(1,128)}) custom-call(s32[64]{0:T(128)} %row_hbm.1, s32[64]{0:T(128)} %src_hbm.1, s32[1]{0:T(128)S(6)} %copy.15.eb_hbm, f32[1,64]{1,0:T(1,128)} %bitcast.10, s32[1,64]{1,0:T(1,128)} %bitcast.9, ...), custom_call_target="tpu_custom_call" | custom-call | tf_op jit(solution)/shard_map/layer/pallas_call | solution.py:681
  64.7 1.5 %pass_through.1 = (bf16[64,512]{1,0:T(8,128)(2,1)}, bf16[32,512]{1,0:T(8,128)(2,1)}, f32[32,256]{1,0:T(8,128)}, f32[32,256]{1,0:T(8,128)}, f32[1,64]{1,0:T(1,128)}) custom-call(bf16[64,512]{1,0:T(8,128)(2,1)} %get-tuple-element.15.refs_0_, bf16[32,512]{1,0:T(8,128)(2,1)} %get-tuple-element.16.refs_1_, f32[32,256]{1,0:T(8,128)} %get-tuple-element.17.refs_2_, ...), custom_call_target="tpu_custom_call" | custom-call | tf_op jit(solution)/shard_map/pass_through/pallas_call | solution.py:685

commit v4 on v3

--- a/solution.py
+++ b/solution.py
@@ -87,7 +87,9 @@
     groups = zs * CORES
     lane_groups = hid // LANES
     tiles = 2 * (cf // 8) * lane_groups
-    per = tiles // groups
+    tiles_half = tiles // CORES
+    per = tiles_half // zs
+    bias_at = tiles_half * 8
     sem_plan = {}
 
     def plan(name, count):
@@ -97,8 +99,8 @@
     for name, count in (
         ("a0", zs - 1), ("a1", ys - 1), ("b0", ys - 1), ("b1", zs - 1), ("c0", ys), ("c1", zs),
         ("halo", 2), ("xq", xs - 1), ("cq", xs - 1), ("ws", xs - 1), ("wn", xs - 1), ("bias", xs - 1),
-        ("agg", xs - 1), ("scaled", xs - 1), ("self", xs - 1), ("hid", xs - 1), ("gx", xs - 1),
-        ("ga", groups - 1), ("gy", ys - 1), ("gz", groups - 1),
+        ("agg", xs - 1), ("scaled", xs - 1), ("hid", xs - 1), ("gl", xs - 1), ("bt", xs - 1),
+        ("gc", 1), ("ga", zs - 1), ("gy", ys - 1), ("gz", groups - 1),
         ("core0", ys), ("core1", zs), ("p0", ys - 1), ("p1", zs - 1), ("r0", zs - 1), ("r1", ys - 1), ("out", 2),
     ):
         plan(name, count)
@@ -120,15 +122,15 @@
         near=((blks, cf + half, LANES), F32), deg=((blks, 8, LANES), F32),
         agg=((blks, cf, LANES), BF16), aq=((xs, cf, LANES), BF16),
         ss=((xs, cf, LANES), BF16), sq=((blks, cf, LANES), BF16),
-        st=((xs, cf, LANES), F32), stq=((blks, cf, LANES), F32),
+        stq=((blks, cf, LANES), F32), gl=((blks, hid, LANES), BF16), bt=((xs, 8, LANES), F32),
         hs=((xs, ch, LANES), BF16), hq=((blks, ch, LANES), BF16),
-        gx=((xs, tiles + 1, 8, LANES), F32), gxr=((xs, tiles + 1, 8, LANES), F32),
-        ga=((groups, per + 1, 8, LANES), F32), gar=((groups, per + 1, 8, LANES), F32),
-        gb=((per + 1, 8, LANES), F32), gyr=((ys, per + 1, 8, LANES), F32),
-        gt=((per, 8, LANES), F32), gzr=((groups, per, 8, LANES), F32),
+        gh=((CORES, bias_at + 8, LANES), F32), ghr=((bias_at + 8, LANES), F32),
+        ga=((zs, per * 8 + lane_groups, LANES), F32), gar=((zs, per * 8 + lane_groups, LANES), F32),
+        gb=((per * 8 + lane_groups, LANES), F32), gyr=((ys, per * 8 + lane_groups, LANES), F32),
+        gt=((per * 8, LANES), F32), gzr=((groups, per * 8, LANES), F32),
         BK=((far, cf, LANES), F32),
-        cs0=((chips, half, LANES), F32), cs1=((chips, half, LANES), F32),
-        cr0=((chips, half, LANES), F32), cr1=((chips, half, LANES), F32),
+        cs0=((chips, half, LANES), BF16), cs1=((chips, half, LANES), BF16),
+        cr0=((chips, half, LANES), BF16), cr1=((chips, half, LANES), BF16),
         ps0=((chips, half, LANES), BF16), ps1=((chips, half, LANES), BF16),
         pr0=((ys, zs, half, LANES), BF16), pr1=((zs, ys, half, LANES), BF16),
         q0=((zs, half, LANES), F32), q1=((ys, half, LANES), F32),
@@ -364,6 +366,8 @@
         row_copy.wait()
         src_copy.wait()
 
+        for one in (a0, a1, halo, *early):
+            one.drain()
         def pass_on0(i):
             b0.arrive(i)
             c0.start(i + 1)
@@ -410,6 +414,8 @@
         agg.start_all()
         s["aq"][x] = s["agg"][x]
         deg_row = s["deg"][x][:1]
+        for one in (b0, b1, c0, c1):
+            one.drain()
         agg.arrive_all()
 
         agg_full = s["aq"][...].reshape(fin, LANES)
@@ -424,31 +430,22 @@
         scaled.start_all()
         s["sq"][x] = s["ss"][x]
 
-        pieces = (dot(x_full, grad_low, 1, 1), dot(agg_full, grad_low, 1, 1))
+        s["gl"][x] = grad_low
+        gl = along_x("gl", lambda p: s["gl"].at[x], lambda q: s["gl"].at[q])
+        gl.start_all()
         bias_row = dot(jnp.ones((8, LANES), F32), grad_pre, 1, 1, lax.Precision.HIGHEST)
         rows8 = lax.broadcasted_iota(jnp.int32, (8, LANES), 0)
         bias_tile = jnp.zeros((8, LANES), F32)
         for l in range(lane_groups):
             bias_tile = jnp.where(rows8 == l, bias_row[:, l * LANES : (l + 1) * LANES], bias_tile)
-        for q in range(xs):
-            t = 0
-            for piece in pieces:
-                for r in range(cf // 8):
-                    for l in range(lane_groups):
-                        at = q * cf + r * 8
-                        s["gx"][q, t] = piece[at : at + 8, l * LANES : (l + 1) * LANES]
-                        t += 1
-            s["gx"][q, tiles] = bias_tile
-        gx = along_x("gx", lambda p: s["gx"].at[p], lambda q: s["gxr"].at[q])
-        gx.start_all()
-        s["gxr"][x] = s["gx"][x]
-        s["st"][...] = dot(s["wsF"][...].reshape(fin, hid), grad_low, 1, 0).reshape(xs, cf, LANES)
+        s["bt"][x] = bias_tile
+        bt = along_x("bt", lambda p: s["bt"].at[x], lambda q: s["bt"].at[q])
+        bt.start_all()
         s["hs"][...] = (pre * sigma).astype(BF16).reshape(xs, ch, LANES)
-        own_term = along_x("self", lambda p: s["st"].at[p], lambda q: s["stq"].at[q])
-        hidden = along_x("hid", lambda p: s["hs"].at[p], lambda q: s["hq"].at[q])
-        s["stq"][x] = s["st"][x]
         s["hq"][x] = s["hs"][x]
 
+        for one in (agg,):
+            one.drain()
         scaled.arrive_all()
 
         wide = min(16, far)
@@ -461,6 +458,28 @@
 
         each(far // wide, back)
 
+        gl.arrive_all()
+        bt.arrive_all()
+        grads = None
+        for b in range(blks):
+            both = jnp.concatenate([s["XT"][b], s["agg"][b]], 0)
+            term = dot(both, s["gl"][b], 1, 1)
+            grads = term if grads is None else grads + term
+        t = 0
+        for w in range(2):
+            for r in range(cf // 8):
+                for l in range(lane_groups):
+                    at = w * cf + r * 8
+                    row = t % tiles_half * 8
+                    s["gh"][t // tiles_half, row : row + 8] = grads[at : at + 8, l * LANES : (l + 1) * LANES]
+                    t += 1
+        bias_sum = s["bt"][0]
+        for q in range(1, xs):
+            bias_sum = bias_sum + s["bt"][q]
+        for k in range(CORES):
+            s["gh"][k, bias_at:] = bias_sum
+        gc = to_core("gc", lambda i: s["gh"].at[o], lambda i: s["ghr"], lambda i: s["ghr"])
+        gc.start(0)
 
         def slot(owner):
             f = inv_s[0, owner]
@@ -470,7 +489,7 @@
             def one(k):
                 at = i * zs + k
                 f, there = slot(at * CORES + o)
-                s["cs0"][at] = s["BK"][f, :half] * there
+                s["cs0"][at] = (s["BK"][f, :half] * there).astype(BF16)
 
             for k in range(zs):
                 one(k)
@@ -479,7 +498,7 @@
         def share1(i):
             for k in range(ys):
                 f, there = slot((k * zs + i) * CORES + o)
-                s["cs1"][i * ys + k] = s["BK"][f, half:] * there
+                s["cs1"][i * ys + k] = (s["BK"][f, half:] * there).astype(BF16)
             core1.start(i)
 
         def of0(ref):
@@ -490,22 +509,8 @@
 
         core0 = to_core("core0", of0(s["cs0"]), of0(s["cr0"]), of0(s["cr0"]))
         core1 = to_core("core1", of1(s["cs1"]), of1(s["cr1"]), of1(s["cr1"]))
+        each(zs, share1)
         each(ys, share0)
-        each(zs, share1)
-
-        gx.arrive_all()
-        for t in range(tiles + 1):
-            total = s["gxr"][0, t]
-            for q in range(1, xs):
-                total = total + s["gxr"][q, t]
-            if t < tiles:
-                s["ga"][t // per, t % per] = total
-            else:
-                for g in range(groups):
-                    s["ga"][g, per] = total
-        ga = along_group("ga", lambda p: s["ga"].at[p], lambda q: s["gar"].at[q])
-        ga.start_all()
-        s["gar"][g_me] = s["ga"][g_me]
 
         spread = [None] * (blks + 2)
         for b in range(blks):
@@ -517,7 +522,19 @@
         for b in range(blks):
             s["inner"][b] = spread[b + 1]
         outward = to_sides("out", s["ho"].at[0], s["ho"].at[1], lambda i: s["hr"].at[i])
+        gc.arrive(0)
+        for k in range(zs):
+            rows = slice(k * per * 8, (k + 1) * per * 8)
+            s["ga"][k, : per * 8] = s["gh"][c, rows] + s["ghr"][rows]
+            bias_rows = slice(bias_at, bias_at + lane_groups)
+            s["ga"][k, per * 8 :] = s["gh"][c, bias_rows] + s["ghr"][bias_rows]
+        ga = along_z("ga", lambda p: s["ga"].at[p], *[lambda q: s["gar"].at[q]] * 2, far_first=True)
+        ga.start_all()
+        s["gar"][z] = s["ga"][z]
         outward.start_all()
+        own_self = s["wsF"][x]
+        for b in range(blks):
+            s["stq"][b] = dot(own_self, s["gl"][b], 1, 0)
 
         p0 = along_y("p0", lambda p: s["ps0"].at[pl.ds(p * zs, zs)], lambda q: s["pr0"].at[q], lambda q: s["pr0"].at[q])
         p1 = along_z("p1", lambda p: s["ps1"].at[pl.ds(p * ys, ys)], lambda q: s["pr1"].at[q], lambda q: s["pr1"].at[q])
@@ -527,27 +544,25 @@
             for k in range(zs):
                 at = i * zs + k
                 f, there = slot(at * CORES + c)
-                s["ps0"][at] = (s["BK"][f, :half] * there + s["cr0"][at]).astype(BF16)
+                s["ps0"][at] = (s["BK"][f, :half] * there + s["cr0"][at].astype(F32)).astype(BF16)
 
         def add1(i):
             core1.arrive(i)
             for k in range(ys):
                 at = i * ys + k
                 f, there = slot((k * zs + i) * CORES + c)
-                s["ps1"][at] = (s["BK"][f, half:] * there + s["cr1"][at]).astype(BF16)
-
+                s["ps1"][at] = (s["BK"][f, half:] * there + s["cr1"][at].astype(F32)).astype(BF16)
+
+        each(zs, add1)
+        p1.start_all()
         each(ys, add0)
         p0.start_all()
-        each(zs, add1)
-        p1.start_all()
         s["pr0"][y] = s["ps0"][pl.ds(y * zs, zs)]
         s["pr1"][z] = s["ps1"][pl.ds(z * ys, ys)]
 
-        own_term.start_all()
-        hidden.start_all()
         ga.arrive_all()
         total = s["gar"][0]
-        for g in range(1, groups):
+        for g in range(1, zs):
             total = total + s["gar"][g]
         s["gb"][...] = total
         gy = along_y("gy", lambda p: s["gb"], *[lambda q: s["gyr"].at[q]] * 2, far_first=True)
@@ -559,50 +574,58 @@
                 total = total + ref[q].astype(F32)
             return total
 
+        for one in (scaled, gl, bt, gc, core0, core1, outward, ga):
+            one.drain()
+        gy.arrive_all()
+        total = s["gyr"][0]
+        for q in range(1, ys):
+            total = total + s["gyr"][q]
+        s["gt"][...] = total[: per * 8]
+        gb_row = jnp.zeros((1, ch), F32)
+        for q in range(xs):
+            at = q * ch
+            row = per * 8 + at // LANES
+            part = total[row : row + 1, at % LANES : at % LANES + ch]
+            gb_row = jnp.where(x == q, part, gb_row)
+        gb_o[...] = gb_row
+        gz = along_group("gz", lambda p: s["gt"], lambda q: s["gzr"].at[q])
+        gz.start_all()
+        s["gzr"][g_me] = total[: per * 8]
+
+        p1.arrive_all()
+        s["q1"][...] = add_up(s["pr1"], zs)
+        r1 = along_y("r1", lambda p: s["q1"].at[p], *[lambda q: s["f1"].at[q]] * 2, far_first=True)
+        r1.start_all()
         p0.arrive_all()
         s["q0"][...] = add_up(s["pr0"], ys)
         r0 = along_z("r0", lambda p: s["q0"].at[p], *[lambda q: s["f0"].at[q]] * 2, far_first=True)
         r0.start_all()
-        p1.arrive_all()
-        s["q1"][...] = add_up(s["pr1"], zs)
-        r1 = along_y("r1", lambda p: s["q1"].at[p], *[lambda q: s["f1"].at[q]] * 2, far_first=True)
-        r1.start_all()
         s["f0"][z] = s["q0"][z]
         s["f1"][y] = s["q1"][y]
 
-        gy.arrive_all()
-        total = s["gyr"][0]
-        for q in range(1, ys):
-            total = total + s["gyr"][q]
-        s["gt"][...] = total[:per]
-        gb_row = jnp.zeros((1, ch), F32)
-        for q in range(xs):
-            at = q * ch
-            part = total[per, at // LANES : at // LANES + 1, at % LANES : at % LANES + ch]
-            gb_row = jnp.where(x == q, part, gb_row)
-        gb_o[...] = gb_row
-        gz = along_group("gz", lambda p: s["gt"], lambda q: s["gzr"].at[q])
-        gz.start_all()
-        s["gzr"][g_me] = total[:per]
-
-        own_term.arrive_all()
-        hidden.arrive_all()
-        for b in range(blks):
-            hid_o[:, b * LANES : (b + 1) * LANES] = s["hq"][b]
-        hid_out = fetch(hid_o, hid_hbm, 12)
+        hidden = along_x("hid", lambda p: s["hs"].at[p], lambda q: s["hq"].at[q])
+        hidden.start_all()
+        for one in (p0, p1, gy):
+            one.drain()
         outward.arrive_all()
         gz.arrive_all()
         t = 0
         for out in (gs_o, gn_o):
             for r in range(cf // 8):
                 for l in range(lane_groups):
-                    out[r * 8 : (r + 1) * 8, l * LANES : (l + 1) * LANES] = s["gzr"][t // per, t % per]
+                    out[r * 8 : (r + 1) * 8, l * LANES : (l + 1) * LANES] = s["gzr"][
+                        t % tiles_half // per * CORES + t // tiles_half, t % per * 8 : t % per * 8 + 8
+                    ]
                     t += 1
         gs_out = fetch(gs_o, gs_hbm, 13)
         gn_out = fetch(gn_o, gn_hbm, 14)
         gb_out = fetch(gb_o, gb_hbm, 15)
+        hidden.arrive_all()
+        for b in range(blks):
+            hid_o[:, b * LANES : (b + 1) * LANES] = s["hq"][b]
+        hid_out = fetch(hid_o, hid_hbm, 12)
+        r1.arrive_all()
         r0.arrive_all()
-        r1.arrive_all()
         far_total = jnp.concatenate([add_up(s["f0"], zs), add_up(s["f1"], ys)], 0)
         for b in range(blks):
             value = s["inner"][b]
@@ -615,10 +638,7 @@
             gf_o[:, b * LANES : (b + 1) * LANES] = value.astype(BF16)
         gf_out = fetch(gf_o, gf_hbm, 16)
 
-        for one in (
-            a0, a1, halo, *early, b0, b1, c0, c1, agg, scaled, gx, own_term, hidden, core0, core1, ga, outward,
-            p0, p1, gy, gz, r0, r1,
-        ):
+        for one in (gz, r0, r1, hidden):
             one.drain()
         for one in (hid_out, gs_out, gn_out, gb_out, gf_out):
             one.wait()

time: 66.4 us -> 64.8 us (0.976)
  Pallas kernels: 64.9 us -> 63.3 us
    pallas_call x1, Pallas kernels: 63.4 us -> 61.8 us  [on_device(): call(far_row, far_src, export_block, bias.reshape(1, -1), far_src.reshape...]
where the time goes in v4:
time: 64.8 us; the launch traced here: 64.6 us
  Pallas kernels  63.3 us (98%)
  between operations  1.29 us (2%)
    pallas_call x1, Pallas kernels, on_device(): call(far_row, far_src, export_block, bias.reshape(1, -1), far_src.reshape...  61.8 us
    pallas_call x1, Pallas kernels, on_device(): hidden, grad_features, grad_self, grad_neigh, grad_bias = finish(*parts)  1.55 us

profile of v4, /device:TPU:1, one launch (start us, length us, event | category | flops | bytes accessed | tf_op | source)
XLA Modules:
  0.0 64.6 jit_solution(15648147161935317909)
XLA Ops:
  1.3 61.8 %layer.1 = (bf16[64,512]{1,0:T(8,128)(2,1)}, bf16[32,512]{1,0:T(8,128)(2,1)}, f32[32,256]{1,0:T(8,128)}, f32[32,256]{1,0:T(8,128)}, f32[1,64]{1,0:T(1,128)}) custom-call(s32[64]{0:T(128)} %row_hbm.1, s32[64]{0:T(128)} %src_hbm.1, s32[1]{0:T(128)S(6)} %copy.15.eb_hbm, f32[1,64]{1,0:T(1,128)} %bitcast.10, s32[1,64]{1,0:T(1,128)} %bitcast.9, ...), custom_call_target="tpu_custom_call" | custom-call | tf_op jit(solution)/shard_map/layer/pallas_call | solution.py:701
  63.1 1.5 %pass_through.1 = (bf16[64,512]{1,0:T(8,128)(2,1)}, bf16[32,512]{1,0:T(8,128)(2,1)}, f32[32,256]{1,0:T(8,128)}, f32[32,256]{1,0:T(8,128)}, f32[1,64]{1,0:T(1,128)}) custom-call(bf16[64,512]{1,0:T(8,128)(2,1)} %get-tuple-element.15.refs_0_, bf16[32,512]{1,0:T(8,128)(2,1)} %get-tuple-element.16.refs_1_, f32[32,256]{1,0:T(8,128)} %get-tuple-element.17.refs_2_, ...), custom_call_target="tpu_custom_call" | custom-call | tf_op jit(solution)/shard_map/pass_through/pallas_call | solution.py:705

commit v5 on v4

--- a/solution.py
+++ b/solution.py
@@ -312,16 +312,16 @@
         def row1(q):
             return e1.at[c, pl.ds(q * ys, ys)]
 
-        b0 = along_y("b0", lambda p: row0(y), row0, row0)
-        b1 = along_z("b1", lambda p: row1(z), row1, row1)
+        b0 = along_y("b0", lambda p: row0(y), row0, row0, far_first=True)
+        b1 = along_z("b1", lambda p: row1(z), row1, row1, far_first=True)
 
         def near_y(i):
             i = jnp.int32(i)
-            return lax.rem(y - nearest(jnp.maximum(i - 1, 0), ys) * jnp.minimum(i, 1) + ys, ys)
+            return lax.rem(y - offset(jnp.maximum(i - 1, 0), ys, True) * jnp.minimum(i, 1) + ys, ys)
 
         def near_z(i):
             i = jnp.int32(i)
-            return lax.rem(z - nearest(jnp.maximum(i - 1, 0), zs) * jnp.minimum(i, 1) + zs, zs)
+            return lax.rem(z - offset(jnp.maximum(i - 1, 0), zs, True) * jnp.minimum(i, 1) + zs, zs)
 
         c0 = to_core(
             "c0", lambda i: row0(near_y(i)), lambda i: row0(near_y(i)), lambda i: e0.at[o, pl.ds(near_y(i) * zs, zs)]
@@ -536,8 +536,8 @@
         for b in range(blks):
             s["stq"][b] = dot(own_self, s["gl"][b], 1, 0)
 
-        p0 = along_y("p0", lambda p: s["ps0"].at[pl.ds(p * zs, zs)], lambda q: s["pr0"].at[q], lambda q: s["pr0"].at[q])
-        p1 = along_z("p1", lambda p: s["ps1"].at[pl.ds(p * ys, ys)], lambda q: s["pr1"].at[q], lambda q: s["pr1"].at[q])
+        p0 = along_y("p0", lambda p: s["ps0"].at[pl.ds(p * zs, zs)], *[lambda q: s["pr0"].at[q]] * 2, far_first=True)
+        p1 = along_z("p1", lambda p: s["ps1"].at[pl.ds(p * ys, ys)], *[lambda q: s["pr1"].at[q]] * 2, far_first=True)
 
         def add0(i):
             core0.arrive(i)

time: 64.8 us -> 63.7 us (0.983)
  Pallas kernels: 63.3 us -> 62.2 us
    pallas_call x1, Pallas kernels: 61.8 us -> 60.6 us  [on_device(): call(far_row, far_src, export_block, bias.reshape(1, -1), far_src.reshape...]
where the time goes in v5:
time: 63.7 us; the launch traced here: 63.4 us
  Pallas kernels  62.2 us (98%)
  between operations  1.29 us (2%)
    pallas_call x1, Pallas kernels, on_device(): call(far_row, far_src, export_block, bias.reshape(1, -1), far_src.reshape...  60.6 us
    pallas_call x1, Pallas kernels, on_device(): hidden, grad_features, grad_self, grad_neigh, grad_bias = finish(*parts)  1.55 us

profile of v5, /device:TPU:1, one launch (start us, length us, event | category | flops | bytes accessed | tf_op | source)
XLA Modules:
  0.0 63.4 jit_solution(7997134887825727777)
XLA Ops:
  1.3 60.6 %layer.1 = (bf16[64,512]{1,0:T(8,128)(2,1)}, bf16[32,512]{1,0:T(8,128)(2,1)}, f32[32,256]{1,0:T(8,128)}, f32[32,256]{1,0:T(8,128)}, f32[1,64]{1,0:T(1,128)}) custom-call(s32[64]{0:T(128)} %row_hbm.1, s32[64]{0:T(128)} %src_hbm.1, s32[1]{0:T(128)S(6)} %copy.15.eb_hbm, f32[1,64]{1,0:T(1,128)} %bitcast.10, s32[1,64]{1,0:T(1,128)} %bitcast.9, ...), custom_call_target="tpu_custom_call" | custom-call | tf_op jit(solution)/shard_map/layer/pallas_call | solution.py:701
  61.9 1.5 %pass_through.1 = (bf16[64,512]{1,0:T(8,128)(2,1)}, bf16[32,512]{1,0:T(8,128)(2,1)}, f32[32,256]{1,0:T(8,128)}, f32[32,256]{1,0:T(8,128)}, f32[1,64]{1,0:T(1,128)}) custom-call(bf16[64,512]{1,0:T(8,128)(2,1)} %get-tuple-element.15.refs_0_, bf16[32,512]{1,0:T(8,128)(2,1)} %get-tuple-element.16.refs_1_, f32[32,256]{1,0:T(8,128)} %get-tuple-element.17.refs_2_, ...), custom_call_target="tpu_custom_call" | custom-call | tf_op jit(solution)/shard_map/pass_through/pallas_call | solution.py:705
